TPU v7x, 32 devices: a whole 2x2x4 slice. The times are simulated.
32 devices in a mesh: rows: 8 (over z, core), cols: 4 (over y, x).
Axes of the slice: x: 2, y: 2, z: 4, core: 2. Of those that a mesh axis runs over, the one named last changes fastest.
Arguments:
- item_factors: bfloat16 [128, 16384], P('cols', 'rows'), may hold values from -0.5 to 0.5
- send_list: int32 [8, 8, 32], P('rows'), may hold values from 0 to 2047, as said below
- obs_slot: int32 [64, 8192], P(None, 'rows'), may hold values from 0 to 255, as said below
- obs_weight: float32 [64, 8192], P(None, 'rows'), may hold values from 0.1 to 10
- rating: float32 [64, 8192], P(None, 'rows'), may hold values from -6 to 6
- counts: int32 [8192], P('rows'), may hold values from 5 to 64, as said below
Outputs:
- user_factors: float32 [128, 8192], P('cols', 'rows')
Inputs may be any that keep to these rules, and one draw needn't show every extreme that they name: `send_list`: for each source and destination block the 32 indices are distinct. `obs_slot`: the live slots of one user name distinct positions. `counts`: in every draw some user has 64 live slots.
All inputs are finite; a program needn't handle non-finite values.
Results may differ from a plain program's by a relative error of at most 0.0007.
Values may be sent and summed in bfloat16 or wider, within the bound.
No kernel may reach another device: no remote copies, remote signals or barrier semaphores. Data moves between devices by JAX's collectives and lax.ppermute only.
A program may use at most 64 MiB of HBM per device.

v0:
```python
import jax
import jax.numpy as jnp
from jax import lax
from jax.sharding import PartitionSpec as P

ITERS = 4


ridge_scale = 0.05


def update(tiles, weighted, ridge, direction, along, length_sq, norm_now, solution, residual):
    scaled = weighted * along
    image = jnp.sum(tiles * scaled[None], axis=1) + ridge * direction
    curvature = jnp.sum(scaled * along, axis=0) + ridge * length_sq
    step_size = norm_now / curvature
    return (solution + step_size * direction, residual - step_size * image)


def squared_norm(values):
    partial_sum = jnp.sum(values * values, axis=0)
    return lax.psum(partial_sum, "cols")


def conjugate_plain(tiles, weighted, rating, ridge):
    target = jnp.sum(tiles * (weighted * rating)[None], axis=1)
    solution = jnp.zeros_like(target)
    residual = target
    direction = target
    norm_now = squared_norm(target)
    for iteration in range(ITERS):
        along_part = jnp.sum(tiles * direction[:, None, :], axis=0)
        length_part = jnp.sum(direction * direction, axis=0)
        along, length_sq = lax.psum((along_part, length_part), "cols")
        solution, residual = update(
            tiles, weighted, ridge, direction, along, length_sq, norm_now, solution, residual
        )
        if iteration + 1 < ITERS:
            norm_next = squared_norm(residual)
            direction = residual + norm_next / norm_now * direction
            norm_now = norm_next
    return solution


def shards(item_factors, send_list, obs_slot, obs_weight, rating, counts):
    columns = item_factors.shape[0]
    row_count = lax.axis_size("rows")
    slot_count = send_list.shape[2]
    outgoing = jnp.take(item_factors, send_list.reshape(-1), axis=1).reshape(
        columns, row_count, slot_count
    )
    arrived = lax.all_to_all(outgoing, "rows", split_axis=1, concat_axis=1, tiled=True).reshape(
        columns, row_count * slot_count
    )
    tiles = jnp.take(arrived, obs_slot, axis=1)
    present = jnp.arange(obs_slot.shape[0], dtype=jnp.int32)[:, None] < counts[None, :]
    weighted = jnp.where(present, obs_weight, jnp.float32(0.0))
    ridge = ridge_scale * counts.astype(jnp.float32)
    return conjugate_plain(tiles, weighted, rating, ridge)


def solution(mesh):
    placed = (
        P("cols", "rows"),
        P("rows", None, None),
        P(None, "rows"),
        P(None, "rows"),
        P(None, "rows"),
        P("rows"),
    )
    return jax.shard_map(
        shards, mesh=mesh, in_specs=placed, out_specs=P("cols", "rows"), check_vma=False
    )
```

profile of v0, /device:TPU:0, one launch (start us, length us, event | category | flops | bytes accessed | tf_op | source)
XLA Modules:
  0.0 639.1 jit_solution(1347853026237816553)
XLA Ops:
  6.5 0.8 reshape.270
  7.3 0.7 compare_and_fusion.1
  8.0 1.2 copy.14
  9.2 0.9 gather_fusion
  10.0 0.1 fusion.18
  10.2 0.7 reshape.290
  10.9 6.3 all-to-all-start
  17.2 0.0 all-reduce.5.cloned.1.call-start
  17.2 1.0 fusion.10
  18.3 1.1 fusion.14
  19.4 1.0 compare_and_fusion
  20.4 2.4 all-to-all-done
  22.9 0.1 reshape.291
  23.0 227.5 %gather_fusion.1 = bf16[65536,32]{1,0:T(8,128)(2,1)} fusion(bf16[32,256]{0,1:T(8,128)(2,1)S(1)} %bitcast.41, s32[65536]{0:T(1024)S(1)} %broadcast_clamp_fusion), kind=kCustom, calls=%fused_computation.1 | custom fusion | bytes 8650752 | tf_op jit(solution)/shard_map/jit(_take)/gather | solution.py:55
  250.4 0.0 copy-start
  250.5 0.0 copy-start.1
  250.5 0.0 copy-start.2
  250.5 21.5 %fusion = f32[32,1024]{0,1:T(8,128)S(1)} fusion(f32[64,1024]{1,0:T(8,128)S(1)} %fusion.14, bf16[64,1024,32]{2,1,0:T(8,128)(2,1)} %bitcast.42, pred[64,1024]{1,0:T(8,128)(4,1)S(1)} %compare_and_fusion), kind=kLoop, calls=%fused_computation.10 | loop fusion | flops 8355840 | bytes 4653056 | tf_op jit(solution)/shard_map/reduce_sum | solution.py:26
  272.0 0.0 copy-done
  272.0 21.8 %fusion.1 = f32[64,1024]{1,0:T(8,128)} fusion(f32[32,1024]{0,1:T(8,128)S(1)} %fusion, bf16[64,1024,32]{2,1,0:T(8,128)(2,1)S(1)} %bitcast.49, pred[64,1024]{1,0:T(8,128)(4,1)S(1)} %compare_and_fusion), kind=kLoop, calls=%fused_computation.11 | loop fusion | flops 8323072 | bytes 4653056 | tf_op jit(solution)/shard_map/reduce_sum | solution.py:32
  293.8 0.0 all-reduce.5.cloned.1.call-update
  293.9 0.0 all-reduce.7.cloned.1.call-start
  293.9 0.2 copy.15
  294.1 0.2 multiply_reduce_fusion
  294.3 10.0 %psum.80 = f32[1024]{0:T(1024)S(1)} all-reduce(f32[1024]{0:T(1024)S(1)} %multiply_reduce_fusion), channel_id=1, replica_groups=mesh['rows'=8,'cols'=4] {'cols'}, use_global_device_ids=true, to_apply=%region_2.3 | all-reduce | flops 1024 | bytes 8192 | tf_op jit(solution)/shard_map/psum | solution.py:22
  304.3 31.7 %all-reduce.5.cloned.1.call-done = f32[64,1024]{1,0:T(8,128)} async-done(((f32[64,1024]{1,0:T(8,128)}), f32[64,1024]{1,0:T(8,128)}) %all-reduce.5.cloned.1.call-update) | async-done | bytes 262160 | tf_op jit(solution)/shard_map/psum | solution.py:34
  336.0 0.0 copy-done.1
  336.0 0.0 copy-done.2
  336.0 1.0 multiply_reduce_fusion.3
  337.0 21.4 %fusion.2 = f32[32,1024]{0,1:T(8,128)S(1)} fusion(f32[64,1024]{1,0:T(8,128)S(1)} %get-tuple-element.18, bf16[64,1024,32]{2,1,0:T(8,128)(2,1)} %bitcast.43, pred[64,1024]{1,0:T(8,128)(4,1)S(1)} %compare_and_fusion), kind=kLoop, calls=%fused_computation.12 | loop fusion | flops 8355840 | bytes 4653056 | tf_op jit(solution)/shard_map/reduce_sum | solution.py:14
  358.4 0.2 copy.17
  358.7 8.9 %psum.82 = f32[1024]{0:T(1024)S(1)} all-reduce(f32[1024]{0:T(1024)S(1)} %multiply_reduce_fusion.9), channel_id=1, replica_groups=mesh['rows'=8,'cols'=4] {'cols'}, use_global_device_ids=true, to_apply=%region_8.9 | all-reduce | flops 1024 | bytes 8192 | tf_op jit(solution)/shard_map/psum | solution.py:22
  367.6 0.1 multiply_reduce_fusion.8
  367.7 0.2 copy.20
  367.9 23.3 %fusion.3 = f32[64,1024]{1,0:T(8,128)} fusion(f32[32,1024]{0,1:T(8,128)S(1)} %copy.20, bf16[64,1024,32]{2,1,0:T(8,128)(2,1)} %bitcast.44, pred[64,1024]{1,0:T(8,128)(4,1)S(1)} %compare_and_fusion), kind=kLoop, calls=%fused_computation.13 | loop fusion | flops 8323072 | bytes 4653056 | tf_op jit(solution)/shard_map/reduce_sum | solution.py:32
  391.2 0.0 all-reduce.7.cloned.1.call-update
  391.2 0.0 all-reduce.9.cloned.1.call-start
  391.2 8.9 %psum.84 = f32[1024]{0:T(1024)S(1)} all-reduce(f32[1024]{0:T(1024)S(1)} %get-tuple-element.13), channel_id=1, replica_groups=mesh['rows'=8,'cols'=4] {'cols'}, use_global_device_ids=true, to_apply=%region_13.14 | all-reduce | flops 1024 | bytes 8192 | tf_op jit(solution)/shard_map/psum | solution.py:34
  400.1 34.2 %all-reduce.7.cloned.1.call-done = f32[64,1024]{1,0:T(8,128)} async-done(((f32[64,1024]{1,0:T(8,128)}), f32[64,1024]{1,0:T(8,128)}) %all-reduce.7.cloned.1.call-update) | async-done | bytes 262160 | tf_op jit(solution)/shard_map/psum | solution.py:34
  434.3 1.0 multiply_reduce_fusion.2
  435.3 21.4 %fusion.4 = f32[32,1024]{0,1:T(8,128)S(1)} fusion(f32[64,1024]{1,0:T(8,128)S(1)} %get-tuple-element.16, bf16[64,1024,32]{2,1,0:T(8,128)(2,1)} %bitcast.45, pred[64,1024]{1,0:T(8,128)(4,1)S(1)} %compare_and_fusion), kind=kLoop, calls=%fused_computation.14 | loop fusion | flops 8355840 | bytes 4653056 | tf_op jit(solution)/shard_map/reduce_sum | solution.py:14
  456.7 0.2 copy.21
  456.9 0.1 multiply_reduce_fusion.7
  457.0 8.9 %psum.85 = f32[1024]{0:T(1024)S(1)} all-reduce(f32[1024]{0:T(1024)S(1)} %get-tuple-element.11), channel_id=1, replica_groups=mesh['rows'=8,'cols'=4] {'cols'}, use_global_device_ids=true, to_apply=%region_16.17 | all-reduce | flops 1024 | bytes 8192 | tf_op jit(solution)/shard_map/psum | solution.py:22
  465.9 0.2 copy.22
  466.1 23.3 %fusion.5 = f32[64,1024]{1,0:T(8,128)} fusion(f32[32,1024]{0,1:T(8,128)S(1)} %copy.22, bf16[64,1024,32]{2,1,0:T(8,128)(2,1)} %bitcast.46, pred[64,1024]{1,0:T(8,128)(4,1)S(1)} %compare_and_fusion), kind=kLoop, calls=%fused_computation.15 | loop fusion | flops 8323072 | bytes 4653056 | tf_op jit(solution)/shard_map/reduce_sum | solution.py:32
  489.4 0.0 all-reduce.9.cloned.1.call-update
  489.5 0.0 all-reduce.11.cloned.1.call-start
  489.5 8.9 %psum.87 = f32[1024]{0:T(1024)S(1)} all-reduce(f32[1024]{0:T(1024)S(1)} %get-tuple-element.7), channel_id=1, replica_groups=mesh['rows'=8,'cols'=4] {'cols'}, use_global_device_ids=true, to_apply=%region_21.22 | all-reduce | flops 1024 | bytes 8192 | tf_op jit(solution)/shard_map/psum | solution.py:34
  498.4 34.1 %all-reduce.9.cloned.1.call-done = f32[64,1024]{1,0:T(8,128)} async-done(((f32[64,1024]{1,0:T(8,128)}), f32[64,1024]{1,0:T(8,128)}) %all-reduce.9.cloned.1.call-update) | async-done | bytes 262160 | tf_op jit(solution)/shard_map/psum | solution.py:34
  532.6 1.0 multiply_reduce_fusion.1
  533.6 21.4 %fusion.6 = f32[32,1024]{0,1:T(8,128)S(1)} fusion(f32[64,1024]{1,0:T(8,128)S(1)} %get-tuple-element.10, bf16[64,1024,32]{2,1,0:T(8,128)(2,1)} %bitcast.47, pred[64,1024]{1,0:T(8,128)(4,1)S(1)} %compare_and_fusion), kind=kLoop, calls=%fused_computation.16 | loop fusion | flops 8355840 | bytes 4653056 | tf_op jit(solution)/shard_map/reduce_sum | solution.py:14
  555.0 0.2 copy.23
  555.2 8.9 %psum.88 = f32[1024]{0:T(1024)S(1)} all-reduce(f32[1024]{0:T(1024)S(1)} %multiply_reduce_fusion.5), channel_id=1, replica_groups=mesh['rows'=8,'cols'=4] {'cols'}, use_global_device_ids=true, to_apply=%region_24.25 | all-reduce | flops 1024 | bytes 8192 | tf_op jit(solution)/shard_map/psum | solution.py:22
  564.2 0.1 multiply_reduce_fusion.4
  564.2 0.2 copy.24
  564.4 23.3 %fusion.7 = f32[64,1024]{1,0:T(8,128)} fusion(f32[32,1024]{0,1:T(8,128)S(1)} %copy.24, bf16[64,1024,32]{2,1,0:T(8,128)(2,1)} %bitcast.48, pred[64,1024]{1,0:T(8,128)(4,1)S(1)} %compare_and_fusion), kind=kLoop, calls=%fused_computation.17 | loop fusion | flops 8323072 | bytes 4653056 | tf_op jit(solution)/shard_map/reduce_sum | solution.py:32
  587.7 0.0 all-reduce.11.cloned.1.call-update
  587.7 8.9 %psum.90 = f32[1024]{0:T(1024)S(1)} all-reduce(f32[1024]{0:T(1024)S(1)} %get-tuple-element.5), channel_id=1, replica_groups=mesh['rows'=8,'cols'=4] {'cols'}, use_global_device_ids=true, to_apply=%region_29.30 | all-reduce | flops 1024 | bytes 8192 | tf_op jit(solution)/shard_map/psum | solution.py:34
  596.6 34.2 %all-reduce.11.cloned.1.call-done = f32[64,1024]{1,0:T(8,128)} async-done(((f32[64,1024]{1,0:T(8,128)}), f32[64,1024]{1,0:T(8,128)}) %all-reduce.11.cloned.1.call-update) | async-done | bytes 262160 | tf_op jit(solution)/shard_map/psum | solution.py:34
  630.8 1.0 fusion.8
  631.9 0.7 multiply_add_fusion
  (14 shorter events, 0.3 us)
Async XLA Ops:
  10.9 12.0 %all-to-all-start = ((bf16[8,2,512]{2,1,0:T(2,128)(2,1)}), bf16[8,2,512]{2,1,0:T(2,128)(2,1)S(1)}, u32[]{:S(2)}, u32[]{:S(2)}) async-start(bf16[8,2,512]{2,1,0:T(2,128)(2,1)} %reshape.290), calls=%async_computation | async-start | bytes 32768 | tf_op jit(solution)/shard_map/all_to_all | solution.py:52
  17.2 318.8 %all-reduce.5.cloned.1.call-start = ((), (), s32[]{:S(2)}) async-start(), calls=%async_computation.1 | async-start | bytes 524288 | tf_op jit(solution)/shard_map/psum | solution.py:34
  250.4 21.5 %copy-start = (bf16[65536,32]{1,0:T(8,128)(2,1)S(1)}, bf16[65536,32]{1,0:T(8,128)(2,1)}, u32[]{:S(2)}) copy-start(bf16[65536,32]{1,0:T(8,128)(2,1)} %gather_fusion.1) | copy-start | bytes 12582916
  250.5 85.6 %copy-start.1 = (f32[64,1024]{1,0:T(8,128)S(1)}, f32[64,1024]{1,0:T(8,128)}, u32[]{:S(2)}) copy-start(f32[64,1024]{1,0:T(8,128)} %param.9) | copy-start | bytes 786436
  250.5 85.6 %copy-start.2 = (s32[1024]{0:T(1024)S(1)}, s32[1024]{0:T(1024)}, u32[]{:S(2)}) copy-start(s32[1024]{0:T(1024)} %param.11) | copy-start | bytes 12292
  293.9 140.4 %all-reduce.7.cloned.1.call-start = ((), (), s32[]{:S(2)}) async-start(), calls=%async_computation.2 | async-start | bytes 524288 | tf_op jit(solution)/shard_map/psum | solution.py:34
  391.2 141.4 %all-reduce.9.cloned.1.call-start = ((), (), s32[]{:S(2)}) async-start(), calls=%async_computation.3 | async-start | bytes 524288 | tf_op jit(solution)/shard_map/psum | solution.py:34
  489.5 141.4 %all-reduce.11.cloned.1.call-start = ((), (), s32[]{:S(2)}) async-start(), calls=%async_computation.4 | async-start | bytes 524288 | tf_op jit(solution)/shard_map/psum | solution.py:34
Sparse Core Ops, SparseCore 0:
  294.0 41.9 all-reduce.4
  391.3 42.9 all-reduce.6
  489.6 42.9 all-reduce.8
  587.9 42.9 all-reduce.10
where the time goes:
time: 640 us; the launch traced here: 639 us
  local copies, waits for them, and re-layouts  232 us (36%)
  other arithmetic  187 us (29%)
  waiting for transfers between devices  137 us (21%)
  blocking collectives  63.5 us (10%)
  between operations  13.3 us (2%)
  starting transfers between devices  6.48 us (1%)
    gather x1, local copies, waits for them, and re-layouts, shards(): tiles = jnp.take(arrived, obs_slot, axis=1)  227 us
    psum x4, waiting for transfers between devices, conjugate_plain(): along, length_sq = lax.psum((along_part, length_part), 'cols')  134 us
    reduce_sum x4, other arithmetic, conjugate_plain(): along_part = jnp.sum(tiles * direction[:, None, :], axis=0)  91.8 us
    reduce_sum x3, other arithmetic, update(): image = jnp.sum(tiles * scaled[None], axis=1) + ridge * direction  64.1 us
    psum x4, blocking collectives, squared_norm(): return lax.psum(partial_sum, 'cols')  36.8 us
    psum x3, blocking collectives, conjugate_plain(): along, length_sq = lax.psum((along_part, length_part), 'cols')  26.7 us
    reduce_sum x1, other arithmetic, conjugate_plain(): target = jnp.sum(tiles * (weighted * rating)[None], axis=1)  21.5 us
  transfers between devices with their start and end apart: 5, of which 5 were waited for; matrix products, arithmetic and copies ran while one was open for 1% of the time, Pallas kernels for 0%

commit v1 on v0

--- a/solution.py
+++ b/solution.py
@@ -1,6 +1,10 @@
+import functools
+
 import jax
 import jax.numpy as jnp
 from jax import lax
+from jax.experimental import pallas as pl
+from jax.experimental.pallas import tpu as pltpu
 from jax.sharding import PartitionSpec as P
 
 ITERS = 4
@@ -42,7 +46,7 @@
     return solution
 
 
-def shards(item_factors, send_list, obs_slot, obs_weight, rating, counts):
+def sparse_shards(item_factors, send_list, obs_slot, obs_weight, rating, counts):
     columns = item_factors.shape[0]
     row_count = lax.axis_size("rows")
     slot_count = send_list.shape[2]
@@ -57,6 +61,176 @@
     weighted = jnp.where(present, obs_weight, jnp.float32(0.0))
     ridge = ridge_scale * counts.astype(jnp.float32)
     return conjugate_plain(tiles, weighted, rating, ridge)
+
+
+def pieces_of(values, count):
+    pieces = []
+    for _ in range(count):
+        piece = values.astype(jnp.bfloat16)
+        pieces.append(piece)
+        values = values - piece.astype(jnp.float32)
+    return jnp.concatenate(pieces, axis=0)
+
+
+def pick_kernel(col_count, factors_ref, list_ref, out_ref):
+    factor_count, items = factors_ref.shape
+    _, row_count, slots = list_ref.shape
+    wanted = jnp.concatenate([list_ref[0, d : d + 1, :] for d in range(row_count)], axis=1)
+    item = lax.broadcasted_iota(jnp.int32, (items, row_count * slots), 0)
+    chosen = (item == wanted).astype(jnp.bfloat16)
+    picked = jnp.dot(factors_ref[...], chosen, preferred_element_type=jnp.float32)
+    group = lax.broadcasted_iota(jnp.int32, (8, 128), 1) // slots
+    for d in range(row_count):
+        start = d * slots
+        base = start // 128 * 128
+        chunk = jnp.zeros((8, 128), jnp.float32)
+        for i in range(factor_count // 8):
+            piece = picked[8 * i : 8 * i + 8, base : base + 128]
+            shift = (slots * i - (start - base)) % 128
+            if shift:
+                piece = pltpu.roll(piece, shift, 1)
+            chunk = jnp.where(group == i, piece, chunk)
+        chunk = chunk.astype(jnp.bfloat16)
+        for c in range(col_count):
+            out_ref[d * col_count + c] = chunk
+
+
+def spread_kernel(slot_ref, weight_ref, rating_ref, counts_ref, w_ref, b_ref, live_slot):
+    obs, users = slot_ref.shape
+    positions = w_ref.shape[0]
+    rows = min(128, positions)
+    order = lax.broadcasted_iota(jnp.int32, (obs, users), 0)
+    live_slot[...] = jnp.where(order < counts_ref[...], slot_ref[...], -1)
+    place = lax.broadcasted_iota(jnp.int32, (rows, users), 0)
+
+    @pl.loop(0, positions // rows)
+    def _(part):
+        start = pl.multiple_of(part * rows, rows)
+        weight = jnp.zeros((rows, users), jnp.float32)
+        value = jnp.zeros((rows, users), jnp.float32)
+        for o in range(obs):
+            here = place == live_slot[o : o + 1, :] - start
+            weight = jnp.where(here, weight_ref[o : o + 1, :], weight)
+            value = jnp.where(here, rating_ref[o : o + 1, :], value)
+        w_ref[pl.ds(start, rows), :] = weight
+        b_ref[pl.ds(start, rows), :] = weight * value
+
+
+def solve_kernel(arrived_ref, w_ref, b_ref, counts_ref, out_ref, twice_t, thrice, slots, col_count):
+    own, users = out_ref.shape
+    positions = w_ref.shape[0]
+    factor_count = own * col_count
+    row_count = positions // slots
+
+    @pl.when(pl.program_id(0) == 0)
+    def _():
+        me = lax.axis_index("cols")
+        group = lax.broadcasted_iota(jnp.int32, (8, 128), 1) // slots
+        per_tile = 128 // slots
+        for j in range(col_count):
+            source = lax.rem(me + j, col_count)
+            chunks = [arrived_ref[s * col_count + source].astype(jnp.float32) for s in range(row_count)]
+            lines = []
+            for i in range(own // 8):
+                tiles = []
+                for first in range(0, row_count, per_tile):
+                    tile = None
+                    for at in range(per_tile):
+                        piece = chunks[first + at]
+                        shift = (slots * (at - i)) % 128
+                        if shift:
+                            piece = pltpu.roll(piece, shift, 1)
+                        tile = piece if tile is None else jnp.where(group == at, piece, tile)
+                    tiles.append(tile)
+                lines.append(jnp.concatenate(tiles, axis=1))
+            block = jnp.concatenate(lines, axis=0)
+            for copy in range(3):
+                thrice[own * j : own * (j + 1), positions * copy : positions * (copy + 1)] = block.astype(jnp.bfloat16)
+        columns_t = jnp.transpose(thrice[:, :positions].astype(jnp.float32)).astype(jnp.bfloat16)
+        for copy in range(2):
+            twice_t[:, factor_count * copy : factor_count * (copy + 1)] = columns_t
+
+    def dot(left, right):
+        return jnp.dot(left, right, preferred_element_type=jnp.float32)
+
+    def total(values):
+        return jnp.sum(values, axis=0, keepdims=True)
+
+    ridge = ridge_scale * counts_ref[...].astype(jnp.float32)
+    residual = dot(thrice[...], pieces_of(b_ref[...], 3))
+    direction = residual
+    norm_now = total(residual * residual)
+    result = jnp.zeros((own, users), jnp.float32)
+    for iteration in range(ITERS):
+        along = dot(twice_t[...], pieces_of(direction, 2))
+        scaled = w_ref[...] * along
+        curvature = total(scaled * along) + ridge * total(direction * direction)
+        step_size = norm_now / curvature
+        result = result + step_size * direction[:own]
+        if iteration + 1 < ITERS:
+            image = dot(thrice[...], pieces_of(scaled, 3)) + ridge * direction
+            residual = residual - step_size * image
+            norm_next = total(residual * residual)
+            direction = residual + norm_next / norm_now * direction
+            norm_now = norm_next
+    out_ref[...] = result
+
+
+def dense_shards(item_factors, send_list, obs_slot, obs_weight, rating, counts):
+    own, items = item_factors.shape
+    row_count = lax.axis_size("rows")
+    col_count = lax.axis_size("cols")
+    slots = send_list.shape[2]
+    obs, users = obs_slot.shape
+    positions = row_count * slots
+    factor_count = own * col_count
+    outgoing = pl.pallas_call(
+        functools.partial(pick_kernel, col_count),
+        out_shape=jax.ShapeDtypeStruct((row_count * col_count, 8, 128), jnp.bfloat16),
+        name="pick",
+    )(item_factors, send_list)
+    arrived = lax.all_to_all(outgoing, ("rows", "cols"), split_axis=0, concat_axis=0, tiled=True)
+    counts = counts.reshape(1, users)
+    wide = 128
+    by_position = jax.ShapeDtypeStruct((positions, users), jnp.float32)
+    weight, value = pl.pallas_call(
+        spread_kernel,
+        out_shape=(by_position, by_position),
+        grid=(users // wide,),
+        in_specs=[pl.BlockSpec((obs, wide), lambda u: (0, u))] * 3 + [pl.BlockSpec((1, wide), lambda u: (0, u))],
+        out_specs=[pl.BlockSpec((positions, wide), lambda u: (0, u))] * 2,
+        scratch_shapes=[pltpu.VMEM((obs, wide), jnp.int32)],
+        cost_estimate=pl.CostEstimate(
+            flops=3 * obs * positions * users, bytes_accessed=(12 * obs + 8 * positions) * users, transcendentals=0
+        ),
+        name="spread",
+    )(obs_slot, obs_weight, rating, counts)
+    wide = 256
+    return pl.pallas_call(
+        functools.partial(solve_kernel, slots=slots, col_count=col_count),
+        out_shape=jax.ShapeDtypeStruct((own, users), jnp.float32),
+        grid=(users // wide,),
+        in_specs=[
+            pl.BlockSpec(arrived.shape, lambda u: (0, 0, 0)),
+            pl.BlockSpec((positions, wide), lambda u: (0, u)),
+            pl.BlockSpec((positions, wide), lambda u: (0, u)),
+            pl.BlockSpec((1, wide), lambda u: (0, u)),
+        ],
+        out_specs=pl.BlockSpec((own, wide), lambda u: (0, u)),
+        scratch_shapes=[
+            pltpu.VMEM((positions, 2 * factor_count), jnp.bfloat16),
+            pltpu.VMEM((factor_count, 3 * positions), jnp.bfloat16),
+        ],
+        compiler_params=pltpu.CompilerParams(vmem_limit_bytes=32 << 20),
+        name="solve",
+    )(arrived, weight, value, counts)
+
+
+def shards(item_factors, send_list, obs_slot, obs_weight, rating, counts):
+    positions = lax.axis_size("rows") * send_list.shape[2]
+    dense = positions <= 512 and 128 % send_list.shape[2] == 0
+    work = dense_shards if dense else sparse_shards
+    return work(item_factors, send_list, obs_slot, obs_weight, rating, counts)
 
 
 def solution(mesh):

time: 640 us -> 36.9 us (0.06)
  local copies, waits for them, and re-layouts: 232 us -> 2.45 us
  other arithmetic: 187 us -> 0 us
  waiting for transfers between devices: 137 us -> 0.01 us
  blocking collectives: 63.5 us -> 0 us
  Pallas kernels: 0 us -> 26.8 us
  between operations: 13.3 us -> 0.03 us
    gather x2 -> x0, local copies, waits for them, and re-layouts: 228 us -> none  [the longest x1 227 us: shards(): tiles = jnp.take(arrived, obs_slot, axis=1)]
    reduce_sum x19 -> x0, other arithmetic: 182 us -> none  [the longest x4 91.8 us: conjugate_plain(): along_part = jnp.sum(tiles * direction[:, None, :], axis=0)]
    psum x4 -> x0, waiting for transfers between devices: 134 us -> none  [conjugate_plain(): along, length_sq = lax.psum((along_part, length_part), 'cols')]
    psum x7 -> x0, blocking collectives: 63.5 us -> none  [the longest x4 36.8 us: squared_norm(): return lax.psum(partial_sum, 'cols')]
    pallas_call x0 -> x3, Pallas kernels: none -> 26.8 us  [the longest x1 16.4 us: dense_shards(): pl.pallas_call(spread_kernel, out_shape=(by_position, by_position), grid=...]
  transfers between devices with their start and end apart: 5 -> 1, of which waited for: 5 -> 0; matrix products, arithmetic and copies ran while one was open for 1% -> 0% of each run, Pallas kernels for 0% -> 45%
where the time goes in v1:
time: 36.9 us; the launch traced here: 36.5 us
  Pallas kernels  26.8 us (73%)
  starting transfers between devices  7.3 us (20%)
  local copies, waits for them, and re-layouts  2.45 us (7%)
    pallas_call x1, Pallas kernels, dense_shards(): pl.pallas_call(spread_kernel, out_shape=(by_position, by_position), grid=...  16.4 us
    pallas_call x1, Pallas kernels, dense_shards(): pl.pallas_call(functools.partial(solve_kernel, slots=slots, col_count=col...  8.35 us
    all_to_all x1, starting transfers between devices, dense_shards(): lax.all_to_all(outgoing, ('rows', 'cols'), split_axis=0, concat_axis=0, t...  7.3 us
    unnamed x6, local copies, waits for them, and re-layouts  2.45 us
    pallas_call x1, Pallas kernels, dense_shards(): pl.pallas_call(functools.partial(pick_kernel, col_count), out_shape=jax.S...  1.98 us
  transfers between devices with their start and end apart: 1, of which 0 were waited for; matrix products, arithmetic and copies ran while one was open for 0% of the time, Pallas kernels for 45%

profile of v1, /device:TPU:0, one launch (start us, length us, event | category | flops | bytes accessed | tf_op | source)
XLA Modules:
  0.0 36.5 jit_solution(3857072211541916079)
XLA Ops:
  0.0 2.0 %pick.1 = bf16[32,8,128]{2,1,0:T(8,128)(2,1)} custom-call(bf16[32,2048]{1,0:T(8,128)(2,1)} %factors_ref.1, s32[1,8,32]{2,1,0:T(8,128)} %list_ref.1), custom_call_target="tpu_custom_call" | custom-call | tf_op jit(solution)/shard_map/pick/pallas_call | solution.py:187
  2.0 7.3 %all-to-all-start = ((bf16[32,8,128]{2,1,0:T(8,128)(2,1)}), bf16[32,8,128]{2,1,0:T(8,128)(2,1)S(1)}, u32[]{:S(2)}, u32[]{:S(2)}) async-start(bf16[32,8,128]{2,1,0:T(8,128)(2,1)} %pick.1), calls=%async_computation | async-start | bytes 131072 | tf_op jit(solution)/shard_map/all_to_all | solution.py:192
  9.3 0.0 copy-start.2
  9.3 16.4 %spread.1 = (f32[256,1024]{1,0:T(8,128)}, f32[256,1024]{1,0:T(8,128)}) custom-call(s32[64,1024]{1,0:T(8,128)} %slot_ref.1, f32[64,1024]{1,0:T(8,128)} %weight_ref.1, f32[64,1024]{1,0:T(8,128)} %rating_ref.1, s32[1,1024]{1,0:T(1,128)} %bitcast.1), custom_call_target="tpu_custom_call" | custom-call | flops 50331648 | bytes 2883584 | tf_op jit(solution)/shard_map/spread/pallas_call | solution.py:196
  25.7 0.0 all-to-all-done.arrived_ref
  25.7 0.0 copy-done.2
  25.8 0.0 copy-start
  25.8 1.2 %copy-done = f32[256,1024]{1,0:T(8,128)S(1)} copy-done((f32[256,1024]{1,0:T(8,128)S(1)}, f32[256,1024]{1,0:T(8,128)}, u32[]{:S(2)}) %copy-start) | copy-done | bytes 1048600
  27.0 0.0 copy-start.1
  27.0 1.2 %copy-done.1 = f32[256,1024]{1,0:T(8,128)S(1)} copy-done((f32[256,1024]{1,0:T(8,128)S(1)}, f32[256,1024]{1,0:T(8,128)}, u32[]{:S(2)}) %copy-start.1) | copy-done | bytes 1048600
  28.2 8.3 %solve.1 = f32[32,1024]{1,0:T(8,128)} custom-call(bf16[32,8,128]{2,1,0:T(8,128)(2,1)S(1)} %all-to-all-done.arrived_ref, f32[256,1024]{1,0:T(8,128)S(1)} %copy-done, f32[256,1024]{1,0:T(8,128)S(1)} %copy-done.1, s32[1,1024]{1,0:T(1,128)S(1)} %bitcast.2), custom_call_target="tpu_custom_call" | custom-call | tf_op jit(solution)/shard_map/solve/pallas_call | solution.py:209
Async XLA Ops:
  2.0 23.8 %all-to-all-start = ((bf16[32,8,128]{2,1,0:T(8,128)(2,1)}), bf16[32,8,128]{2,1,0:T(8,128)(2,1)S(1)}, u32[]{:S(2)}, u32[]{:S(2)}) async-start(bf16[32,8,128]{2,1,0:T(8,128)(2,1)} %pick.1), calls=%async_computation | async-start | bytes 131072 | tf_op jit(solution)/shard_map/all_to_all | solution.py:192
  9.3 16.5 %copy-start.2 = (s32[1024]{0:T(1024)S(1)}, s32[1024]{0:T(1024)}, u32[]{:S(2)}) copy-start(s32[1024]{0:T(1024)} %param.11) | copy-start | bytes 12292
  25.8 1.2 %copy-start = (f32[256,1024]{1,0:T(8,128)S(1)}, f32[256,1024]{1,0:T(8,128)}, u32[]{:S(2)}) copy-start(f32[256,1024]{1,0:T(8,128)} %get-tuple-element.7.w_ref) | copy-start | bytes 3145732
  27.0 1.2 %copy-start.1 = (f32[256,1024]{1,0:T(8,128)S(1)}, f32[256,1024]{1,0:T(8,128)}, u32[]{:S(2)}) copy-start(f32[256,1024]{1,0:T(8,128)} %get-tuple-element.8.b_ref) | copy-start | bytes 3145732

commit v2 on v1

--- a/solution.py
+++ b/solution.py
@@ -95,25 +95,44 @@
             out_ref[d * col_count + c] = chunk
 
 
-def spread_kernel(slot_ref, weight_ref, rating_ref, counts_ref, w_ref, b_ref, live_slot):
+def spread_kernel(slot_ref, weight_ref, rating_ref, counts_ref, w_ref, b_ref, wanted):
     obs, users = slot_ref.shape
     positions = w_ref.shape[0]
-    rows = min(128, positions)
-    order = lax.broadcasted_iota(jnp.int32, (obs, users), 0)
-    live_slot[...] = jnp.where(order < counts_ref[...], slot_ref[...], -1)
-    place = lax.broadcasted_iota(jnp.int32, (rows, users), 0)
-
-    @pl.loop(0, positions // rows)
-    def _(part):
-        start = pl.multiple_of(part * rows, rows)
-        weight = jnp.zeros((rows, users), jnp.float32)
-        value = jnp.zeros((rows, users), jnp.float32)
+    groups = obs // 8
+    levels = groups.bit_length() - 1
+
+    @pl.loop(0, users // 128)
+    def _(tile):
+        lanes = pl.ds(pl.multiple_of(tile * 128, 128), 128)
+        row = lax.broadcasted_iota(jnp.int32, (16, 128), 0)
+        live = counts_ref[:, lanes]
         for o in range(obs):
-            here = place == live_slot[o : o + 1, :] - start
-            weight = jnp.where(here, weight_ref[o : o + 1, :], weight)
-            value = jnp.where(here, rating_ref[o : o + 1, :], value)
-        w_ref[pl.ds(start, rows), :] = weight
-        b_ref[pl.ds(start, rows), :] = weight * value
+            position = jnp.where(live > o, slot_ref[o : o + 1, lanes], -1)
+            wanted[16 * o : 16 * o + 16, :] = (jnp.broadcast_to(position, (16, 128)) - row).astype(jnp.int16)
+        weights = [weight_ref[8 * g : 8 * g + 8, lanes] for g in range(groups)]
+        ratings = [rating_ref[8 * g : 8 * g + 8, lanes] for g in range(groups)]
+        named = [jnp.full((16, 128), obs, jnp.int16)] * (positions // 16)
+        for o in range(obs):
+            offset = wanted[16 * o : 16 * o + 16, :]
+            for k in range(positions // 16):
+                named[k] = jnp.where(offset == jnp.int16(16 * k), jnp.int16(o), named[k])
+        for k in range(positions // 16):
+            both = named[k].astype(jnp.int32)
+            for half in range(2):
+                slot = both[8 * half : 8 * half + 8]
+                within = slot & 7
+                bits = [(slot & (8 << level)) != 0 for level in range(levels)]
+
+                def fetch(blocks):
+                    found = [jnp.take_along_axis(block, within, axis=0) for block in blocks]
+                    for bit in bits:
+                        found = [jnp.where(bit, found[e + 1], found[e]) for e in range(0, len(found), 2)]
+                    return jnp.where(slot < obs, found[0], 0.0)
+
+                weight = fetch(weights)
+                at = slice(16 * k + 8 * half, 16 * k + 8 * half + 8)
+                w_ref[at, lanes] = weight
+                b_ref[at, lanes] = weight * fetch(ratings)
 
 
 def solve_kernel(arrived_ref, w_ref, b_ref, counts_ref, out_ref, twice_t, thrice, slots, col_count):
@@ -122,33 +141,31 @@
     factor_count = own * col_count
     row_count = positions // slots
 
-    @pl.when(pl.program_id(0) == 0)
-    def _():
-        me = lax.axis_index("cols")
-        group = lax.broadcasted_iota(jnp.int32, (8, 128), 1) // slots
-        per_tile = 128 // slots
-        for j in range(col_count):
-            source = lax.rem(me + j, col_count)
-            chunks = [arrived_ref[s * col_count + source].astype(jnp.float32) for s in range(row_count)]
-            lines = []
-            for i in range(own // 8):
-                tiles = []
-                for first in range(0, row_count, per_tile):
-                    tile = None
-                    for at in range(per_tile):
-                        piece = chunks[first + at]
-                        shift = (slots * (at - i)) % 128
-                        if shift:
-                            piece = pltpu.roll(piece, shift, 1)
-                        tile = piece if tile is None else jnp.where(group == at, piece, tile)
-                    tiles.append(tile)
-                lines.append(jnp.concatenate(tiles, axis=1))
-            block = jnp.concatenate(lines, axis=0)
-            for copy in range(3):
-                thrice[own * j : own * (j + 1), positions * copy : positions * (copy + 1)] = block.astype(jnp.bfloat16)
-        columns_t = jnp.transpose(thrice[:, :positions].astype(jnp.float32)).astype(jnp.bfloat16)
-        for copy in range(2):
-            twice_t[:, factor_count * copy : factor_count * (copy + 1)] = columns_t
+    me = lax.axis_index("cols")
+    group = lax.broadcasted_iota(jnp.int32, (8, 128), 1) // slots
+    per_tile = 128 // slots
+    for j in range(col_count):
+        source = lax.rem(me + j, col_count)
+        chunks = [arrived_ref[s * col_count + source].astype(jnp.float32) for s in range(row_count)]
+        lines = []
+        for i in range(own // 8):
+            tiles = []
+            for first in range(0, row_count, per_tile):
+                tile = None
+                for at in range(per_tile):
+                    piece = chunks[first + at]
+                    shift = (slots * (at - i)) % 128
+                    if shift:
+                        piece = pltpu.roll(piece, shift, 1)
+                    tile = piece if tile is None else jnp.where(group == at, piece, tile)
+                tiles.append(tile)
+            lines.append(jnp.concatenate(tiles, axis=1))
+        block = jnp.concatenate(lines, axis=0)
+        for copy in range(3):
+            thrice[own * j : own * (j + 1), positions * copy : positions * (copy + 1)] = block.astype(jnp.bfloat16)
+    columns_t = jnp.transpose(thrice[:, :positions].astype(jnp.float32)).astype(jnp.bfloat16)
+    for copy in range(2):
+        twice_t[:, factor_count * copy : factor_count * (copy + 1)] = columns_t
 
     def dot(left, right):
         return jnp.dot(left, right, preferred_element_type=jnp.float32)
@@ -191,32 +208,25 @@
     )(item_factors, send_list)
     arrived = lax.all_to_all(outgoing, ("rows", "cols"), split_axis=0, concat_axis=0, tiled=True)
     counts = counts.reshape(1, users)
-    wide = 128
-    by_position = jax.ShapeDtypeStruct((positions, users), jnp.float32)
+    vmem = pl.BlockSpec(memory_space=pltpu.VMEM)
+    by_position = pltpu.VMEM((positions, users), jnp.float32)
     weight, value = pl.pallas_call(
         spread_kernel,
         out_shape=(by_position, by_position),
-        grid=(users // wide,),
-        in_specs=[pl.BlockSpec((obs, wide), lambda u: (0, u))] * 3 + [pl.BlockSpec((1, wide), lambda u: (0, u))],
-        out_specs=[pl.BlockSpec((positions, wide), lambda u: (0, u))] * 2,
-        scratch_shapes=[pltpu.VMEM((obs, wide), jnp.int32)],
+        in_specs=[vmem] * 4,
+        out_specs=[vmem] * 2,
+        scratch_shapes=[pltpu.VMEM((16 * obs, 128), jnp.int16)],
+        compiler_params=pltpu.CompilerParams(vmem_limit_bytes=16 << 20),
         cost_estimate=pl.CostEstimate(
             flops=3 * obs * positions * users, bytes_accessed=(12 * obs + 8 * positions) * users, transcendentals=0
         ),
         name="spread",
     )(obs_slot, obs_weight, rating, counts)
-    wide = 256
     return pl.pallas_call(
         functools.partial(solve_kernel, slots=slots, col_count=col_count),
         out_shape=jax.ShapeDtypeStruct((own, users), jnp.float32),
-        grid=(users // wide,),
-        in_specs=[
-            pl.BlockSpec(arrived.shape, lambda u: (0, 0, 0)),
-            pl.BlockSpec((positions, wide), lambda u: (0, u)),
-            pl.BlockSpec((positions, wide), lambda u: (0, u)),
-            pl.BlockSpec((1, wide), lambda u: (0, u)),
-        ],
-        out_specs=pl.BlockSpec((own, wide), lambda u: (0, u)),
+        in_specs=[vmem] * 4,
+        out_specs=vmem,
         scratch_shapes=[
             pltpu.VMEM((positions, 2 * factor_count), jnp.bfloat16),
             pltpu.VMEM((factor_count, 3 * positions), jnp.bfloat16),

time: 36.9 us -> 24.4 us (0.66)
  Pallas kernels: 26.8 us -> 14.9 us
  local copies, waits for them, and re-layouts: 2.45 us -> 1.9 us
    pallas_call x1, Pallas kernels: 16.4 us -> 9.27 us  [dense_shards(): pl.pallas_call(spread_kernel, out_shape=(by_position, by_position), in_sp...]
    pallas_call x1, Pallas kernels: 8.35 us -> 3.58 us  [dense_shards(): pl.pallas_call(functools.partial(solve_kernel, slots=slots, col_count=col...]
    unnamed x6 -> x8, local copies, waits for them, and re-layouts: 2.45 us -> 1.9 us
  transfers between devices with their start and end apart: 1 -> 1, of which waited for: 0 -> 0; matrix products, arithmetic and copies ran while one was open for 0% -> 0% of each run, Pallas kernels for 45% -> 38%
where the time goes in v2:
time: 24.4 us; the launch traced here: 24.1 us
  Pallas kernels  14.9 us (61%)
  starting transfers between devices  7.3 us (30%)
  local copies, waits for them, and re-layouts  1.9 us (8%)
    pallas_call x1, Pallas kernels, dense_shards(): pl.pallas_call(spread_kernel, out_shape=(by_position, by_position), in_sp...  9.27 us
    all_to_all x1, starting transfers between devices, dense_shards(): lax.all_to_all(outgoing, ('rows', 'cols'), split_axis=0, concat_axis=0, t...  7.3 us
    pallas_call x1, Pallas kernels, dense_shards(): pl.pallas_call(functools.partial(solve_kernel, slots=slots, col_count=col...  3.58 us
    pallas_call x1, Pallas kernels, dense_shards(): pl.pallas_call(functools.partial(pick_kernel, col_count), out_shape=jax.S...  2.02 us
    unnamed x8, local copies, waits for them, and re-layouts  1.9 us
  transfers between devices with their start and end apart: 1, of which 0 were waited for; matrix products, arithmetic and copies ran while one was open for 0% of the time, Pallas kernels for 38%

profile of v2, /device:TPU:0, one launch (start us, length us, event | category | flops | bytes accessed | tf_op | source)
XLA Modules:
  0.0 24.1 jit_solution(16610870760671471408)
XLA Ops:
  0.0 0.0 copy-start
  0.0 2.0 %pick.1 = bf16[32,8,128]{2,1,0:T(8,128)(2,1)} custom-call(bf16[32,2048]{1,0:T(8,128)(2,1)} %factors_ref.1, s32[1,8,32]{2,1,0:T(8,128)} %list_ref.1), custom_call_target="tpu_custom_call" | custom-call | tf_op jit(solution)/shard_map/pick/pallas_call | solution.py:204
  2.0 0.0 copy-start.3
  2.0 7.3 %all-to-all-start = ((bf16[32,8,128]{2,1,0:T(8,128)(2,1)}), bf16[32,8,128]{2,1,0:T(8,128)(2,1)S(1)}, u32[]{:S(2)}, u32[]{:S(2)}) async-start(bf16[32,8,128]{2,1,0:T(8,128)(2,1)} %pick.1), calls=%async_computation | async-start | bytes 131072 | tf_op jit(solution)/shard_map/all_to_all | solution.py:209
  9.3 0.0 copy-done
  9.3 0.0 copy-done.3
  9.4 0.0 copy-start.1
  9.4 0.9 %copy-done.1 = f32[64,1024]{1,0:T(8,128)S(1)} copy-done((f32[64,1024]{1,0:T(8,128)S(1)}, f32[64,1024]{1,0:T(8,128)}, u32[]{:S(2)}) %copy-start.1) | copy-done | bytes 262168
  10.3 0.0 copy-start.2
  10.3 0.9 %copy-done.2 = f32[64,1024]{1,0:T(8,128)S(1)} copy-done((f32[64,1024]{1,0:T(8,128)S(1)}, f32[64,1024]{1,0:T(8,128)}, u32[]{:S(2)}) %copy-start.2) | copy-done | bytes 262168
  11.3 9.3 %spread.1 = (f32[256,1024]{1,0:T(8,128)S(1)}, f32[256,1024]{1,0:T(8,128)S(1)}) custom-call(s32[64,1024]{1,0:T(8,128)S(1)} %copy-done, f32[64,1024]{1,0:T(8,128)S(1)} %copy-done.1, f32[64,1024]{1,0:T(8,128)S(1)} %copy-done.2, s32[1,1024]{1,0:T(1,128)S(1)} %bitcast.1), custom_call_target="tpu_custom_call" | custom-call | flops 50331648 | bytes 2883584 | tf_op jit(solution)/shard_map/spread/pallas_call | solution.py:213
  20.5 0.0 all-to-all-done.arrived_ref
  20.5 3.6 %solve.1 = f32[32,1024]{1,0:T(8,128)} custom-call(bf16[32,8,128]{2,1,0:T(8,128)(2,1)S(1)} %all-to-all-done.arrived_ref, f32[256,1024]{1,0:T(8,128)S(1)} %get-tuple-element.7.w_ref, f32[256,1024]{1,0:T(8,128)S(1)} %get-tuple-element.8.b_ref, s32[1,1024]{1,0:T(1,128)S(1)} %bitcast.2), custom_call_target="tpu_custom_call" | custom-call | tf_op jit(solution)/shard_map/solve/pallas_call | solution.py:225
Async XLA Ops:
  0.0 9.3 %copy-start = (s32[64,1024]{1,0:T(8,128)S(1)}, s32[64,1024]{1,0:T(8,128)}, u32[]{:S(2)}) copy-start(s32[64,1024]{1,0:T(8,128)} %slot_ref.1) | copy-start | bytes 786436
  2.0 7.3 %copy-start.3 = (s32[1024]{0:T(1024)S(1)}, s32[1024]{0:T(1024)}, u32[]{:S(2)}) copy-start(s32[1024]{0:T(1024)} %param.11) | copy-start | bytes 12292
  2.0 18.5 %all-to-all-start = ((bf16[32,8,128]{2,1,0:T(8,128)(2,1)}), bf16[32,8,128]{2,1,0:T(8,128)(2,1)S(1)}, u32[]{:S(2)}, u32[]{:S(2)}) async-start(bf16[32,8,128]{2,1,0:T(8,128)(2,1)} %pick.1), calls=%async_computation | async-start | bytes 131072 | tf_op jit(solution)/shard_map/all_to_all | solution.py:209
  9.4 1.0 %copy-start.1 = (f32[64,1024]{1,0:T(8,128)S(1)}, f32[64,1024]{1,0:T(8,128)}, u32[]{:S(2)}) copy-start(f32[64,1024]{1,0:T(8,128)} %weight_ref.1) | copy-start | bytes 786436
  10.3 0.9 %copy-start.2 = (f32[64,1024]{1,0:T(8,128)S(1)}, f32[64,1024]{1,0:T(8,128)}, u32[]{:S(2)}) copy-start(f32[64,1024]{1,0:T(8,128)} %rating_ref.1) | copy-start | bytes 786436

commit v3 on v2

--- a/solution.py
+++ b/solution.py
@@ -72,13 +72,24 @@
     return jnp.concatenate(pieces, axis=0)
 
 
-def pick_kernel(col_count, factors_ref, list_ref, out_ref):
-    factor_count, items = factors_ref.shape
-    _, row_count, slots = list_ref.shape
-    wanted = jnp.concatenate([list_ref[0, d : d + 1, :] for d in range(row_count)], axis=1)
-    item = lax.broadcasted_iota(jnp.int32, (items, row_count * slots), 0)
-    chosen = (item == wanted).astype(jnp.bfloat16)
-    picked = jnp.dot(factors_ref[...], chosen, preferred_element_type=jnp.float32)
+def pick_kernel(col_count, factors_ref, list_ref, out_ref, factors, wanted, chosen, arrived):
+    factor_count, items = factors.shape
+    _, row_count, slots = wanted.shape
+    list_copy = pltpu.make_async_copy(list_ref, wanted, arrived.at[0])
+    factors_copy = pltpu.make_async_copy(factors_ref, factors, arrived.at[1])
+    list_copy.start()
+    factors_copy.start()
+    item = lax.broadcasted_iota(jnp.int32, (items, 128), 0).astype(jnp.int16)
+    list_copy.wait()
+    per_tile = 128 // slots
+    for first in range(0, row_count, per_tile):
+        line = jnp.concatenate([wanted[0, d : d + 1, :] for d in range(first, first + per_tile)], axis=1)
+        line = jnp.broadcast_to(line, (16, 128)).astype(jnp.int16)
+        line = jnp.concatenate([line] * (items // 16), axis=0)
+        at = first * slots
+        chosen[:, at : at + 128] = jnp.where(item == line, jnp.bfloat16(1), jnp.bfloat16(0))
+    factors_copy.wait()
+    picked = jnp.dot(factors[...], chosen[...], preferred_element_type=jnp.float32)
     group = lax.broadcasted_iota(jnp.int32, (8, 128), 1) // slots
     for d in range(row_count):
         start = d * slots
@@ -95,47 +106,74 @@
             out_ref[d * col_count + c] = chunk
 
 
-def spread_kernel(slot_ref, weight_ref, rating_ref, counts_ref, w_ref, b_ref, wanted):
+def spread_kernel(
+    slot_hbm, weight_hbm, rating_hbm, counts_ref, w_ref, b_ref, ridge_ref, slot_ref, weight_ref, rating_ref, wanted, named, arrived
+):
     obs, users = slot_ref.shape
     positions = w_ref.shape[0]
     groups = obs // 8
     levels = groups.bit_length() - 1
+    rows = 32
+    copies = [
+        pltpu.make_async_copy(source, target, arrived.at[at])
+        for at, (source, target) in enumerate(
+            ((slot_hbm, slot_ref), (weight_hbm, weight_ref), (rating_hbm, rating_ref))
+        )
+    ]
+    for copy in copies:
+        copy.start()
+    ridge_ref[...] = ridge_scale * counts_ref[...].astype(jnp.float32)
+    copies[0].wait()
 
     @pl.loop(0, users // 128)
     def _(tile):
         lanes = pl.ds(pl.multiple_of(tile * 128, 128), 128)
-        row = lax.broadcasted_iota(jnp.int32, (16, 128), 0)
+        row = lax.broadcasted_iota(jnp.int32, (rows, 128), 0)
+        for o in range(obs):
+            position = jnp.broadcast_to(slot_ref[o : o + 1, lanes], (rows, 128))
+            wanted[rows * o : rows * (o + 1), :] = (position - 128).astype(jnp.int8)
+        places = [(row + (rows * k - 128)).astype(jnp.int8) for k in range(positions // rows)]
+        found = [jnp.full((rows, 128), obs, jnp.int8) for _ in places]
+        for o in reversed(range(obs)):
+            position = wanted[rows * o : rows * (o + 1), :]
+            found = [jnp.where(position == place, jnp.int8(o), last) for place, last in zip(places, found)]
+        for k, slot in enumerate(found):
+            named[rows * k : rows * (k + 1), lanes] = slot
+
+    for copy in copies[1:]:
+        copy.wait()
+
+    @pl.loop(0, users // 128)
+    def _(tile):
+        lanes = pl.ds(pl.multiple_of(tile * 128, 128), 128)
         live = counts_ref[:, lanes]
-        for o in range(obs):
-            position = jnp.where(live > o, slot_ref[o : o + 1, lanes], -1)
-            wanted[16 * o : 16 * o + 16, :] = (jnp.broadcast_to(position, (16, 128)) - row).astype(jnp.int16)
         weights = [weight_ref[8 * g : 8 * g + 8, lanes] for g in range(groups)]
         ratings = [rating_ref[8 * g : 8 * g + 8, lanes] for g in range(groups)]
-        named = [jnp.full((16, 128), obs, jnp.int16)] * (positions // 16)
-        for o in range(obs):
-            offset = wanted[16 * o : 16 * o + 16, :]
-            for k in range(positions // 16):
-                named[k] = jnp.where(offset == jnp.int16(16 * k), jnp.int16(o), named[k])
-        for k in range(positions // 16):
-            both = named[k].astype(jnp.int32)
-            for half in range(2):
-                slot = both[8 * half : 8 * half + 8]
+        for k in range(positions // rows):
+            slots = named[rows * k : rows * (k + 1), lanes].astype(jnp.int32)
+            values = []
+            for at in range(0, rows, 8):
+                slot = slots[at : at + 8]
                 within = slot & 7
                 bits = [(slot & (8 << level)) != 0 for level in range(levels)]
 
                 def fetch(blocks):
-                    found = [jnp.take_along_axis(block, within, axis=0) for block in blocks]
+                    picked = [jnp.take_along_axis(block, within, axis=0) for block in blocks]
                     for bit in bits:
-                        found = [jnp.where(bit, found[e + 1], found[e]) for e in range(0, len(found), 2)]
-                    return jnp.where(slot < obs, found[0], 0.0)
-
-                weight = fetch(weights)
-                at = slice(16 * k + 8 * half, 16 * k + 8 * half + 8)
-                w_ref[at, lanes] = weight
-                b_ref[at, lanes] = weight * fetch(ratings)
-
-
-def solve_kernel(arrived_ref, w_ref, b_ref, counts_ref, out_ref, twice_t, thrice, slots, col_count):
+                        picked = [jnp.where(bit, picked[e + 1], picked[e]) for e in range(0, len(picked), 2)]
+                    return picked[0]
+
+                weight = jnp.where(slot < live, fetch(weights), 0.0)
+                w_ref[rows * k + at : rows * k + at + 8, lanes] = weight
+                values.append(weight * fetch(ratings))
+            values = jnp.concatenate(values, axis=0)
+            for piece in range(2):
+                part = values.astype(jnp.bfloat16)
+                b_ref[positions * piece + rows * k : positions * piece + rows * (k + 1), lanes] = part
+                values = values - part.astype(jnp.float32)
+
+
+def solve_kernel(arrived_ref, w_ref, b_ref, ridge_ref, out_ref, twice_t, twice, slots, col_count):
     own, users = out_ref.shape
     positions = w_ref.shape[0]
     factor_count = own * col_count
@@ -161,9 +199,9 @@
                 tiles.append(tile)
             lines.append(jnp.concatenate(tiles, axis=1))
         block = jnp.concatenate(lines, axis=0)
-        for copy in range(3):
-            thrice[own * j : own * (j + 1), positions * copy : positions * (copy + 1)] = block.astype(jnp.bfloat16)
-    columns_t = jnp.transpose(thrice[:, :positions].astype(jnp.float32)).astype(jnp.bfloat16)
+        for copy in range(2):
+            twice[own * j : own * (j + 1), positions * copy : positions * (copy + 1)] = block.astype(jnp.bfloat16)
+    columns_t = jnp.transpose(twice[:, :positions].astype(jnp.float32)).astype(jnp.bfloat16)
     for copy in range(2):
         twice_t[:, factor_count * copy : factor_count * (copy + 1)] = columns_t
 
@@ -173,19 +211,23 @@
     def total(values):
         return jnp.sum(values, axis=0, keepdims=True)
 
-    ridge = ridge_scale * counts_ref[...].astype(jnp.float32)
-    residual = dot(thrice[...], pieces_of(b_ref[...], 3))
+    ridge = ridge_ref[...]
+    residual = dot(twice[...], b_ref[...])
     direction = residual
     norm_now = total(residual * residual)
     result = jnp.zeros((own, users), jnp.float32)
     for iteration in range(ITERS):
         along = dot(twice_t[...], pieces_of(direction, 2))
         scaled = w_ref[...] * along
-        curvature = total(scaled * along) + ridge * total(direction * direction)
+        last = iteration + 1 == ITERS
+        if last:
+            curvature = total(scaled * along) + ridge * total(direction * direction)
+        else:
+            image = dot(twice[...], pieces_of(scaled, 2)) + ridge * direction
+            curvature = total(image * direction)
         step_size = norm_now / curvature
         result = result + step_size * direction[:own]
-        if iteration + 1 < ITERS:
-            image = dot(thrice[...], pieces_of(scaled, 3)) + ridge * direction
+        if not last:
             residual = residual - step_size * image
             norm_next = total(residual * residual)
             direction = residual + norm_next / norm_now * direction
@@ -201,27 +243,51 @@
     obs, users = obs_slot.shape
     positions = row_count * slots
     factor_count = own * col_count
+    vmem = pl.BlockSpec(memory_space=pltpu.VMEM)
+    hbm = pl.BlockSpec(memory_space=pltpu.HBM)
+
+    def in_hbm(array):
+        return pltpu.with_memory_space_constraint(array, pltpu.HBM)
+
     outgoing = pl.pallas_call(
         functools.partial(pick_kernel, col_count),
-        out_shape=jax.ShapeDtypeStruct((row_count * col_count, 8, 128), jnp.bfloat16),
+        out_shape=pltpu.VMEM((row_count * col_count, 8, 128), jnp.bfloat16),
+        in_specs=[hbm] * 2,
+        out_specs=vmem,
+        scratch_shapes=[
+            pltpu.VMEM(item_factors.shape, item_factors.dtype),
+            pltpu.VMEM(send_list.shape, send_list.dtype),
+            pltpu.VMEM((items, positions), jnp.bfloat16),
+            pltpu.SemaphoreType.DMA((2,)),
+        ],
+        compiler_params=pltpu.CompilerParams(vmem_limit_bytes=4 << 20),
         name="pick",
-    )(item_factors, send_list)
+    )(*map(in_hbm, (item_factors, send_list)))
     arrived = lax.all_to_all(outgoing, ("rows", "cols"), split_axis=0, concat_axis=0, tiled=True)
     counts = counts.reshape(1, users)
-    vmem = pl.BlockSpec(memory_space=pltpu.VMEM)
-    by_position = pltpu.VMEM((positions, users), jnp.float32)
-    weight, value = pl.pallas_call(
+    weight, value, ridge = pl.pallas_call(
         spread_kernel,
-        out_shape=(by_position, by_position),
-        in_specs=[vmem] * 4,
-        out_specs=[vmem] * 2,
-        scratch_shapes=[pltpu.VMEM((16 * obs, 128), jnp.int16)],
-        compiler_params=pltpu.CompilerParams(vmem_limit_bytes=16 << 20),
+        out_shape=(
+            pltpu.VMEM((positions, users), jnp.float32),
+            pltpu.VMEM((2 * positions, users), jnp.bfloat16),
+            pltpu.VMEM((1, users), jnp.float32),
+        ),
+        in_specs=[hbm] * 3 + [vmem],
+        out_specs=[vmem] * 3,
+        scratch_shapes=[
+            pltpu.VMEM((obs, users), jnp.int32),
+            pltpu.VMEM((obs, users), jnp.float32),
+            pltpu.VMEM((obs, users), jnp.float32),
+            pltpu.VMEM((32 * obs, 128), jnp.int8),
+            pltpu.VMEM((positions, users), jnp.int8),
+            pltpu.SemaphoreType.DMA((3,)),
+        ],
+        compiler_params=pltpu.CompilerParams(vmem_limit_bytes=8 << 20),
         cost_estimate=pl.CostEstimate(
             flops=3 * obs * positions * users, bytes_accessed=(12 * obs + 8 * positions) * users, transcendentals=0
         ),
         name="spread",
-    )(obs_slot, obs_weight, rating, counts)
+    )(*map(in_hbm, (obs_slot, obs_weight, rating)), counts)
     return pl.pallas_call(
         functools.partial(solve_kernel, slots=slots, col_count=col_count),
         out_shape=jax.ShapeDtypeStruct((own, users), jnp.float32),
@@ -229,16 +295,17 @@
         out_specs=vmem,
         scratch_shapes=[
             pltpu.VMEM((positions, 2 * factor_count), jnp.bfloat16),
-            pltpu.VMEM((factor_count, 3 * positions), jnp.bfloat16),
+            pltpu.VMEM((factor_count, 2 * positions), jnp.bfloat16),
         ],
         compiler_params=pltpu.CompilerParams(vmem_limit_bytes=32 << 20),
         name="solve",
-    )(arrived, weight, value, counts)
+    )(arrived, weight, value, ridge)
 
 
 def shards(item_factors, send_list, obs_slot, obs_weight, rating, counts):
     positions = lax.axis_size("rows") * send_list.shape[2]
-    dense = positions <= 512 and 128 % send_list.shape[2] == 0
+    obs = obs_slot.shape[0]
+    dense = positions <= 256 and 128 % send_list.shape[2] == 0 and obs <= 64 and obs & (obs - 1) == 0
     work = dense_shards if dense else sparse_shards
     return work(item_factors, send_list, obs_slot, obs_weight, rating, counts)
 

time: 24.4 us -> 20.2 us (0.83)
  Pallas kernels: 14.9 us -> 9.88 us
  waiting for transfers between devices: 0.01 us -> 2.72 us
  local copies, waits for them, and re-layouts: 1.9 us -> 0.01 us
    pallas_call x2, Pallas kernels: 11.3 us -> 6.73 us  [the longest x1 4.76 us: dense_shards(): pl.pallas_call(spread_kernel, out_shape=(pltpu.VMEM((positions, users), j...]
    all_to_all x1, waiting for transfers between devices: 0.01 us -> 2.72 us  [dense_shards(): lax.all_to_all(outgoing, ('rows', 'cols'), split_axis=0, concat_axis=0, t...]
    unnamed x8 -> x2, local copies, waits for them, and re-layouts: 1.9 us -> 0.01 us
    pallas_call x1, Pallas kernels: 3.58 us -> 3.14 us  [dense_shards(): pl.pallas_call(functools.partial(solve_kernel, slots=slots, col_count=col...]
  transfers between devices with their start and end apart: 1 -> 1, of which waited for: 0 -> 1; matrix products, arithmetic and copies ran while one was open for 0% -> 0% of each run, Pallas kernels for 38% -> 24%
where the time goes in v3:
time: 20.2 us; the launch traced here: 20 us
  Pallas kernels  9.88 us (49%)
  starting transfers between devices  7.3 us (36%)
  waiting for transfers between devices  2.72 us (13%)
    all_to_all x1, starting transfers between devices, dense_shards(): lax.all_to_all(outgoing, ('rows', 'cols'), split_axis=0, concat_axis=0, t...  7.3 us
    pallas_call x1, Pallas kernels, dense_shards(): pl.pallas_call(spread_kernel, out_shape=(pltpu.VMEM((positions, users), j...  4.76 us
    pallas_call x1, Pallas kernels, dense_shards(): pl.pallas_call(functools.partial(solve_kernel, slots=slots, col_count=col...  3.14 us
    all_to_all x1, waiting for transfers between devices, dense_shards(): lax.all_to_all(outgoing, ('rows', 'cols'), split_axis=0, concat_axis=0, t...  2.72 us
    pallas_call x1, Pallas kernels, dense_shards(): pl.pallas_call(functools.partial(pick_kernel, col_count), out_shape=pltpu...  1.98 us
  transfers between devices with their start and end apart: 1, of which 1 were waited for; matrix products, arithmetic and copies ran while one was open for 0% of the time, Pallas kernels for 24%

profile of v3, /device:TPU:0, one launch (start us, length us, event | category | flops | bytes accessed | tf_op | source)
XLA Modules:
  0.0 20.0 jit_solution(13824979933315672391)
XLA Ops:
  0.0 2.0 %pick.1 = bf16[32,8,128]{2,1,0:T(8,128)(2,1)} custom-call(bf16[32,2048]{1,0:T(8,128)(2,1)} %factors_ref.1, s32[1,8,32]{2,1,0:T(8,128)} %list_ref.1), custom_call_target="tpu_custom_call" | custom-call | tf_op jit(solution)/shard_map/pick/pallas_call | solution.py:252
  2.0 0.0 copy-start
  2.0 7.3 %all-to-all-start = ((bf16[32,8,128]{2,1,0:T(8,128)(2,1)}), bf16[32,8,128]{2,1,0:T(8,128)(2,1)S(1)}, u32[]{:S(2)}, u32[]{:S(2)}) async-start(bf16[32,8,128]{2,1,0:T(8,128)(2,1)} %pick.1), calls=%async_computation | async-start | bytes 131072 | tf_op jit(solution)/shard_map/all_to_all | solution.py:266
  9.3 0.0 copy-done
  9.3 4.8 %spread.1 = (f32[256,1024]{1,0:T(8,128)S(1)}, bf16[512,1024]{1,0:T(8,128)(2,1)S(1)}, f32[1,1024]{1,0:T(1,128)S(1)}) custom-call(s32[64,1024]{1,0:T(8,128)} %slot_hbm.1, f32[64,1024]{1,0:T(8,128)} %weight_hbm.1, f32[64,1024]{1,0:T(8,128)} %rating_hbm.1, s32[1,1024]{1,0:T(1,128)S(1)} %bitcast.1), custom_call_target="tpu_custom_call" | custom-call | flops 50331648 | bytes 2883584 | tf_op jit(solution)/shard_map/spread/pallas_call | solution.py:268
  14.1 2.7 %all-to-all-done.arrived_ref = bf16[32,8,128]{2,1,0:T(8,128)(2,1)S(1)} async-done(((bf16[32,8,128]{2,1,0:T(8,128)(2,1)}), bf16[32,8,128]{2,1,0:T(8,128)(2,1)S(1)}, u32[]{:S(2)}, u32[]{:S(2)}) %all-to-all-start) | async-done | bytes 65568 | tf_op jit(solution)/shard_map/all_to_all | solution.py:266
  16.8 3.1 %solve.1 = f32[32,1024]{1,0:T(8,128)} custom-call(bf16[32,8,128]{2,1,0:T(8,128)(2,1)S(1)} %all-to-all-done.arrived_ref, f32[256,1024]{1,0:T(8,128)S(1)} %get-tuple-element.8.w_ref, bf16[512,1024]{1,0:T(8,128)(2,1)S(1)} %get-tuple-element.9.b_ref, f32[1,1024]{1,0:T(1,128)S(1)} %get-tuple-element.10.ridge_ref), custom_call_target="tpu_custom_call" | custom-call | tf_op jit(solution)/shard_map/solve/pallas_call | solution.py:291
Async XLA Ops:
  2.0 7.3 %copy-start = (s32[1024]{0:T(1024)S(1)}, s32[1024]{0:T(1024)}, u32[]{:S(2)}) copy-start(s32[1024]{0:T(1024)} %param.11) | copy-start | bytes 12292
  2.0 14.8 %all-to-all-start = ((bf16[32,8,128]{2,1,0:T(8,128)(2,1)}), bf16[32,8,128]{2,1,0:T(8,128)(2,1)S(1)}, u32[]{:S(2)}, u32[]{:S(2)}) async-start(bf16[32,8,128]{2,1,0:T(8,128)(2,1)} %pick.1), calls=%async_computation | async-start | bytes 131072 | tf_op jit(solution)/shard_map/all_to_all | solution.py:266

commit v4 on v3

--- a/solution.py
+++ b/solution.py
@@ -72,42 +72,63 @@
     return jnp.concatenate(pieces, axis=0)
 
 
-def pick_kernel(col_count, factors_ref, list_ref, out_ref, factors, wanted, chosen, arrived):
+def swap_blocks(parts, width, wanted):
+    count = 128 // width
+    block = lax.broadcasted_iota(jnp.int32, (8, 128), 1) // width
+    turned = []
+    for shift in range(count):
+        line = None
+        for at in range(count):
+            source = (at + shift) % count
+            if source < len(parts):
+                line = parts[source] if line is None else jnp.where(block == at, parts[source], line)
+        turned.append(pltpu.roll(line, width * shift, 1) if shift else line)
+    results = []
+    for a in range(wanted):
+        result = turned[-a % count]
+        for b in range(1, len(parts)):
+            result = jnp.where(block == b, turned[(b - a) % count], result)
+        results.append(result)
+    return results
+
+
+def pick_kernel(col_count, factors_ref, list_ref, out_ref, factors, wanted, ready, arrived, left):
     factor_count, items = factors.shape
     _, row_count, slots = wanted.shape
     list_copy = pltpu.make_async_copy(list_ref, wanted, arrived.at[0])
     factors_copy = pltpu.make_async_copy(factors_ref, factors, arrived.at[1])
     list_copy.start()
     factors_copy.start()
-    item = lax.broadcasted_iota(jnp.int32, (items, 128), 0).astype(jnp.int16)
+    within = lax.broadcasted_iota(jnp.int32, (128, row_count * slots), 0)
     list_copy.wait()
+    item = jnp.concatenate([wanted[0, d : d + 1, :] for d in range(row_count)], axis=1)
+    chosen = jnp.where(within == (item & 127), jnp.float32(1), jnp.float32(0)).astype(jnp.bfloat16)
+    factors_copy.wait()
+    groups = items // 128
+    stacked = jnp.concatenate([factors[:, 128 * g : 128 * (g + 1)] for g in range(groups)], axis=0)
+    found = jnp.dot(stacked, chosen, preferred_element_type=jnp.float32)
+    picked = found[:factor_count]
+    for g in range(1, groups):
+        picked = jnp.where(item >> 7 == g, found[factor_count * g : factor_count * (g + 1)], picked)
     per_tile = 128 // slots
+    chunk_rows = 8 * col_count
+    copies = []
     for first in range(0, row_count, per_tile):
-        line = jnp.concatenate([wanted[0, d : d + 1, :] for d in range(first, first + per_tile)], axis=1)
-        line = jnp.broadcast_to(line, (16, 128)).astype(jnp.int16)
-        line = jnp.concatenate([line] * (items // 16), axis=0)
-        at = first * slots
-        chosen[:, at : at + 128] = jnp.where(item == line, jnp.bfloat16(1), jnp.bfloat16(0))
-    factors_copy.wait()
-    picked = jnp.dot(factors[...], chosen[...], preferred_element_type=jnp.float32)
-    group = lax.broadcasted_iota(jnp.int32, (8, 128), 1) // slots
-    for d in range(row_count):
-        start = d * slots
-        base = start // 128 * 128
-        chunk = jnp.zeros((8, 128), jnp.float32)
-        for i in range(factor_count // 8):
-            piece = picked[8 * i : 8 * i + 8, base : base + 128]
-            shift = (slots * i - (start - base)) % 128
-            if shift:
-                piece = pltpu.roll(piece, shift, 1)
-            chunk = jnp.where(group == i, piece, chunk)
-        chunk = chunk.astype(jnp.bfloat16)
-        for c in range(col_count):
-            out_ref[d * col_count + c] = chunk
+        lines = picked[:, first * slots : first * slots + 128]
+        parts = [lines[8 * i : 8 * i + 8] for i in range(factor_count // 8)]
+        for d, chunk in enumerate(swap_blocks(parts, slots, per_tile), first):
+            chunk = jnp.concatenate([chunk] * col_count, axis=0).astype(jnp.bfloat16)
+            ready[chunk_rows * d : chunk_rows * (d + 1), :] = chunk
+        part = pl.ds(chunk_rows * first, chunk_rows * per_tile)
+        copy = pltpu.make_async_copy(ready.at[part], out_ref.at[part], left.at[len(copies)])
+        copy.start()
+        copies.append(copy)
+    for copy in copies:
+        copy.wait()
 
 
 def spread_kernel(
-    slot_hbm, weight_hbm, rating_hbm, counts_ref, w_ref, b_ref, ridge_ref, slot_ref, weight_ref, rating_ref, wanted, named, arrived
+    slot_hbm, weight_hbm, rating_hbm, counts_ref, w_ref, b_ref, slot_ref, weight_ref, rating_ref, wanted, named, arrived
 ):
     obs, users = slot_ref.shape
     positions = w_ref.shape[0]
@@ -122,7 +143,6 @@
     ]
     for copy in copies:
         copy.start()
-    ridge_ref[...] = ridge_scale * counts_ref[...].astype(jnp.float32)
     copies[0].wait()
 
     @pl.loop(0, users // 128)
@@ -147,6 +167,7 @@
     def _(tile):
         lanes = pl.ds(pl.multiple_of(tile * 128, 128), 128)
         live = counts_ref[:, lanes]
+        scale = 1.0 / (ridge_scale * live.astype(jnp.float32))
         weights = [weight_ref[8 * g : 8 * g + 8, lanes] for g in range(groups)]
         ratings = [rating_ref[8 * g : 8 * g + 8, lanes] for g in range(groups)]
         for k in range(positions // rows):
@@ -163,7 +184,7 @@
                         picked = [jnp.where(bit, picked[e + 1], picked[e]) for e in range(0, len(picked), 2)]
                     return picked[0]
 
-                weight = jnp.where(slot < live, fetch(weights), 0.0)
+                weight = jnp.where(slot < live, fetch(weights) * scale, 0.0)
                 w_ref[rows * k + at : rows * k + at + 8, lanes] = weight
                 values.append(weight * fetch(ratings))
             values = jnp.concatenate(values, axis=0)
@@ -173,32 +194,23 @@
                 values = values - part.astype(jnp.float32)
 
 
-def solve_kernel(arrived_ref, w_ref, b_ref, ridge_ref, out_ref, twice_t, twice, slots, col_count):
+def solve_kernel(arrived_ref, w_ref, b_ref, out_ref, unpacked, twice_t, twice, image_ref, slots, col_count):
     own, users = out_ref.shape
     positions = w_ref.shape[0]
     factor_count = own * col_count
     row_count = positions // slots
 
+    unpacked[...] = arrived_ref[...].astype(jnp.float32)
     me = lax.axis_index("cols")
-    group = lax.broadcasted_iota(jnp.int32, (8, 128), 1) // slots
     per_tile = 128 // slots
     for j in range(col_count):
         source = lax.rem(me + j, col_count)
-        chunks = [arrived_ref[s * col_count + source].astype(jnp.float32) for s in range(row_count)]
-        lines = []
-        for i in range(own // 8):
-            tiles = []
-            for first in range(0, row_count, per_tile):
-                tile = None
-                for at in range(per_tile):
-                    piece = chunks[first + at]
-                    shift = (slots * (at - i)) % 128
-                    if shift:
-                        piece = pltpu.roll(piece, shift, 1)
-                    tile = piece if tile is None else jnp.where(group == at, piece, tile)
-                tiles.append(tile)
-            lines.append(jnp.concatenate(tiles, axis=1))
-        block = jnp.concatenate(lines, axis=0)
+        chunks = [unpacked[pl.ds(8 * (s * col_count + source), 8), :] for s in range(row_count)]
+        tiles = [
+            jnp.concatenate(swap_blocks(chunks[first : first + per_tile], slots, own // 8), axis=0)
+            for first in range(0, row_count, per_tile)
+        ]
+        block = jnp.concatenate(tiles, axis=1)
         for copy in range(2):
             twice[own * j : own * (j + 1), positions * copy : positions * (copy + 1)] = block.astype(jnp.bfloat16)
     columns_t = jnp.transpose(twice[:, :positions].astype(jnp.float32)).astype(jnp.bfloat16)
@@ -209,30 +221,44 @@
         return jnp.dot(left, right, preferred_element_type=jnp.float32)
 
     def total(values):
+        while values.shape[0] > 8:
+            half = values.shape[0] // 2
+            values = values[:half] + values[half:]
         return jnp.sum(values, axis=0, keepdims=True)
 
-    ridge = ridge_ref[...]
-    residual = dot(twice[...], b_ref[...])
-    direction = residual
-    norm_now = total(residual * residual)
-    result = jnp.zeros((own, users), jnp.float32)
-    for iteration in range(ITERS):
+    def target(lanes):
+        return dot(twice[...], b_ref[:, lanes])
+
+    def reach(lanes, direction, last=False):
         along = dot(twice_t[...], pieces_of(direction, 2))
-        scaled = w_ref[...] * along
-        last = iteration + 1 == ITERS
+        scaled = w_ref[:, lanes] * along
         if last:
-            curvature = total(scaled * along) + ridge * total(direction * direction)
-        else:
-            image = dot(twice[...], pieces_of(scaled, 2)) + ridge * direction
-            curvature = total(image * direction)
-        step_size = norm_now / curvature
+            return total(scaled * along)
+        image_ref[:, lanes] = dot(twice[...], pieces_of(scaled, 2))
+        return image_ref[:, lanes] + direction
+
+    def advance(state, image):
+        residual, direction, norm_now, length, result = state
+        step_size = norm_now / total(image * direction)
         result = result + step_size * direction[:own]
-        if not last:
-            residual = residual - step_size * image
-            norm_next = total(residual * residual)
-            direction = residual + norm_next / norm_now * direction
-            norm_now = norm_next
-    out_ref[...] = result
+        residual = residual - step_size * image
+        norm_next = total(residual * residual)
+        ratio = norm_next / norm_now
+        return residual, residual + ratio * direction, norm_next, norm_next + ratio * ratio * length, result
+
+    def finish(lanes, state, square):
+        _, direction, norm_now, length, result = state
+        out_ref[:, lanes] = result + norm_now / (square + length) * direction[:own]
+
+    def begin(residual):
+        norm_now = total(residual * residual)
+        return residual, residual, norm_now, norm_now, jnp.zeros((own, residual.shape[1]), jnp.float32)
+
+    everyone = slice(0, users)
+    state = begin(target(everyone))
+    for _ in range(ITERS - 1):
+        state = advance(state, reach(everyone, state[1]))
+    finish(everyone, state, reach(everyone, state[1], True))
 
 
 def dense_shards(item_factors, send_list, obs_slot, obs_weight, rating, counts):
@@ -249,31 +275,32 @@
     def in_hbm(array):
         return pltpu.with_memory_space_constraint(array, pltpu.HBM)
 
+    chunk_rows = 8 * row_count * col_count
     outgoing = pl.pallas_call(
         functools.partial(pick_kernel, col_count),
-        out_shape=pltpu.VMEM((row_count * col_count, 8, 128), jnp.bfloat16),
+        out_shape=jax.ShapeDtypeStruct((chunk_rows, 128), jnp.bfloat16),
         in_specs=[hbm] * 2,
-        out_specs=vmem,
+        out_specs=hbm,
         scratch_shapes=[
             pltpu.VMEM(item_factors.shape, item_factors.dtype),
             pltpu.VMEM(send_list.shape, send_list.dtype),
-            pltpu.VMEM((items, positions), jnp.bfloat16),
+            pltpu.VMEM((chunk_rows, 128), jnp.bfloat16),
             pltpu.SemaphoreType.DMA((2,)),
+            pltpu.SemaphoreType.DMA((positions // 128,)),
         ],
         compiler_params=pltpu.CompilerParams(vmem_limit_bytes=4 << 20),
         name="pick",
     )(*map(in_hbm, (item_factors, send_list)))
     arrived = lax.all_to_all(outgoing, ("rows", "cols"), split_axis=0, concat_axis=0, tiled=True)
     counts = counts.reshape(1, users)
-    weight, value, ridge = pl.pallas_call(
+    weight, value = pl.pallas_call(
         spread_kernel,
         out_shape=(
             pltpu.VMEM((positions, users), jnp.float32),
             pltpu.VMEM((2 * positions, users), jnp.bfloat16),
-            pltpu.VMEM((1, users), jnp.float32),
         ),
         in_specs=[hbm] * 3 + [vmem],
-        out_specs=[vmem] * 3,
+        out_specs=[vmem] * 2,
         scratch_shapes=[
             pltpu.VMEM((obs, users), jnp.int32),
             pltpu.VMEM((obs, users), jnp.float32),
@@ -291,21 +318,25 @@
     return pl.pallas_call(
         functools.partial(solve_kernel, slots=slots, col_count=col_count),
         out_shape=jax.ShapeDtypeStruct((own, users), jnp.float32),
-        in_specs=[vmem] * 4,
+        in_specs=[vmem] * 3,
         out_specs=vmem,
         scratch_shapes=[
+            pltpu.VMEM((chunk_rows, 128), jnp.float32),
             pltpu.VMEM((positions, 2 * factor_count), jnp.bfloat16),
             pltpu.VMEM((factor_count, 2 * positions), jnp.bfloat16),
+            pltpu.VMEM((factor_count, users), jnp.float32),
         ],
         compiler_params=pltpu.CompilerParams(vmem_limit_bytes=32 << 20),
         name="solve",
-    )(arrived, weight, value, ridge)
+    )(arrived, weight, value)
 
 
 def shards(item_factors, send_list, obs_slot, obs_weight, rating, counts):
     positions = lax.axis_size("rows") * send_list.shape[2]
     obs = obs_slot.shape[0]
-    dense = positions <= 256 and 128 % send_list.shape[2] == 0 and obs <= 64 and obs & (obs - 1) == 0
+    own = item_factors.shape[0]
+    packs = own % 8 == 0 and own // 8 * send_list.shape[2] <= 128
+    dense = packs and positions <= 256 and positions % 128 == 0 and 128 % send_list.shape[2] == 0 and obs <= 64 and obs & (obs - 1) == 0
     work = dense_shards if dense else sparse_shards
     return work(item_factors, send_list, obs_slot, obs_weight, rating, counts)
 

time: 20.2 us -> 20 us (0.990)
  no operation moved by 1% of the time
where the time goes in v4:
time: 20 us; the launch traced here: 19.8 us
  Pallas kernels  9.79 us (49%)
  starting transfers between devices  7.3 us (36%)
  waiting for transfers between devices  2.68 us (13%)
    all_to_all x1, starting transfers between devices, dense_shards(): lax.all_to_all(outgoing, ('rows', 'cols'), split_axis=0, concat_axis=0, t...  7.3 us
    pallas_call x1, Pallas kernels, dense_shards(): pl.pallas_call(spread_kernel, out_shape=(pltpu.VMEM((positions, users), j...  4.8 us
    pallas_call x1, Pallas kernels, dense_shards(): pl.pallas_call(functools.partial(solve_kernel, slots=slots, col_count=col...  3.12 us
    all_to_all x1, waiting for transfers between devices, dense_shards(): lax.all_to_all(outgoing, ('rows', 'cols'), split_axis=0, concat_axis=0, t...  2.68 us
    pallas_call x1, Pallas kernels, dense_shards(): pl.pallas_call(functools.partial(pick_kernel, col_count), out_shape=jax.S...  1.87 us
  transfers between devices with their start and end apart: 1, of which 1 were waited for; matrix products, arithmetic and copies ran while one was open for 0% of the time, Pallas kernels for 24%

profile of v4, /device:TPU:0, one launch (start us, length us, event | category | flops | bytes accessed | tf_op | source)
XLA Modules:
  0.0 19.8 jit_solution(5677164300116608618)
XLA Ops:
  0.0 1.9 %pick.1 = bf16[256,128]{1,0:T(8,128)(2,1)} custom-call(bf16[32,2048]{1,0:T(8,128)(2,1)} %factors_ref.1, s32[1,8,32]{2,1,0:T(8,128)} %list_ref.1), custom_call_target="tpu_custom_call" | custom-call | tf_op jit(solution)/shard_map/pick/pallas_call | solution.py:279
  1.9 0.0 copy-start
  1.9 7.3 %all-to-all-start = ((bf16[32,8,128]{2,1,0:T(8,128)(2,1)}), bf16[32,8,128]{2,1,0:T(8,128)(2,1)S(1)}, u32[]{:S(2)}, u32[]{:S(2)}) async-start(bf16[32,8,128]{2,1,0:T(8,128)(2,1)} %bitcast), calls=%async_computation | async-start | bytes 131072 | tf_op jit(solution)/shard_map/all_to_all | solution.py:294
  9.2 0.0 copy-done
  9.2 4.8 %spread.1 = (f32[256,1024]{1,0:T(8,128)S(1)}, bf16[512,1024]{1,0:T(8,128)(2,1)S(1)}) custom-call(s32[64,1024]{1,0:T(8,128)} %slot_hbm.1, f32[64,1024]{1,0:T(8,128)} %weight_hbm.1, f32[64,1024]{1,0:T(8,128)} %rating_hbm.1, s32[1,1024]{1,0:T(1,128)S(1)} %bitcast.4), custom_call_target="tpu_custom_call" | custom-call | flops 50331648 | bytes 2883584 | tf_op jit(solution)/shard_map/spread/pallas_call | solution.py:296
  14.0 2.7 %all-to-all-done = bf16[32,8,128]{2,1,0:T(8,128)(2,1)S(1)} async-done(((bf16[32,8,128]{2,1,0:T(8,128)(2,1)}), bf16[32,8,128]{2,1,0:T(8,128)(2,1)S(1)}, u32[]{:S(2)}, u32[]{:S(2)}) %all-to-all-start) | async-done | bytes 65568 | tf_op jit(solution)/shard_map/all_to_all | solution.py:294
  16.7 3.1 %solve.1 = f32[32,1024]{1,0:T(8,128)} custom-call(bf16[256,128]{1,0:T(8,128)(2,1)S(1)} %bitcast.3, f32[256,1024]{1,0:T(8,128)S(1)} %get-tuple-element.7.w_ref, bf16[512,1024]{1,0:T(8,128)(2,1)S(1)} %get-tuple-element.8.b_ref), custom_call_target="tpu_custom_call" | custom-call | tf_op jit(solution)/shard_map/solve/pallas_call | solution.py:318
Async XLA Ops:
  1.9 7.3 %copy-start = (s32[1024]{0:T(1024)S(1)}, s32[1024]{0:T(1024)}, u32[]{:S(2)}) copy-start(s32[1024]{0:T(1024)} %param.11) | copy-start | bytes 12292
  1.9 14.8 %all-to-all-start = ((bf16[32,8,128]{2,1,0:T(8,128)(2,1)}), bf16[32,8,128]{2,1,0:T(8,128)(2,1)S(1)}, u32[]{:S(2)}, u32[]{:S(2)}) async-start(bf16[32,8,128]{2,1,0:T(8,128)(2,1)} %bitcast), calls=%async_computation | async-start | bytes 131072 | tf_op jit(solution)/shard_map/all_to_all | solution.py:294

commit v5 on v4

--- a/solution.py
+++ b/solution.py
@@ -1,4 +1,5 @@
 import functools
+import math
 
 import jax
 import jax.numpy as jnp
@@ -190,7 +191,8 @@
             values = jnp.concatenate(values, axis=0)
             for piece in range(2):
                 part = values.astype(jnp.bfloat16)
-                b_ref[positions * piece + rows * k : positions * piece + rows * (k + 1), lanes] = part
+                at = rows * k // 128 * 256 + 128 * piece + rows * k % 128
+                b_ref[at : at + rows, lanes] = part
                 values = values - part.astype(jnp.float32)
 
 
@@ -211,11 +213,15 @@
             for first in range(0, row_count, per_tile)
         ]
         block = jnp.concatenate(tiles, axis=1)
+        for part in range(positions // 128):
+            for copy in range(2):
+                at = 256 * part + 128 * copy
+                twice[own * j : own * (j + 1), at : at + 128] = block[:, 128 * part : 128 * part + 128].astype(jnp.bfloat16)
+    for part in range(positions // 128):
+        columns = twice[:, 256 * part : 256 * part + 128].astype(jnp.float32)
+        columns_t = jnp.transpose(columns).astype(jnp.bfloat16)
         for copy in range(2):
-            twice[own * j : own * (j + 1), positions * copy : positions * (copy + 1)] = block.astype(jnp.bfloat16)
-    columns_t = jnp.transpose(twice[:, :positions].astype(jnp.float32)).astype(jnp.bfloat16)
-    for copy in range(2):
-        twice_t[:, factor_count * copy : factor_count * (copy + 1)] = columns_t
+            twice_t[128 * part : 128 * part + 128, factor_count * copy : factor_count * (copy + 1)] = columns_t
 
     def dot(left, right):
         return jnp.dot(left, right, preferred_element_type=jnp.float32)
@@ -229,12 +235,17 @@
     def target(lanes):
         return dot(twice[...], b_ref[:, lanes])
 
-    def reach(lanes, direction, last=False):
+    def look(lanes, direction):
         along = dot(twice_t[...], pieces_of(direction, 2))
-        scaled = w_ref[:, lanes] * along
-        if last:
-            return total(scaled * along)
-        image_ref[:, lanes] = dot(twice[...], pieces_of(scaled, 2))
+        parts = [slice(at, at + 128) for at in range(0, positions, 128)]
+        return [(along[part], w_ref[part, lanes] * along[part]) for part in parts]
+
+    def square(views):
+        return sum(total(scaled * along) for along, scaled in views)
+
+    def back(lanes, views, direction):
+        pieces = jnp.concatenate([pieces_of(scaled, 2) for _, scaled in views], axis=0)
+        image_ref[:, lanes] = dot(twice[...], pieces)
         return image_ref[:, lanes] + direction
 
     def advance(state, image):
@@ -254,11 +265,14 @@
         norm_now = total(residual * residual)
         return residual, residual, norm_now, norm_now, jnp.zeros((own, residual.shape[1]), jnp.float32)
 
-    everyone = slice(0, users)
-    state = begin(target(everyone))
+    width = math.gcd(users, 256)
+    groups = [slice(at, at + width) for at in range(0, users, width)]
+    states = [begin(target(lanes)) for lanes in groups]
     for _ in range(ITERS - 1):
-        state = advance(state, reach(everyone, state[1]))
-    finish(everyone, state, reach(everyone, state[1], True))
+        images = [back(lanes, look(lanes, state[1]), state[1]) for lanes, state in zip(groups, states)]
+        states = [advance(state, image) for state, image in zip(states, images)]
+    for lanes, state in zip(groups, states):
+        finish(lanes, state, square(look(lanes, state[1])))
 
 
 def dense_shards(item_factors, send_list, obs_slot, obs_weight, rating, counts):

time: 20 us -> 19.8 us (0.990)
  Pallas kernels: 9.79 us -> 9.53 us
    pallas_call x1, Pallas kernels: 3.12 us -> 2.86 us  [dense_shards(): pl.pallas_call(functools.partial(solve_kernel, slots=slots, col_count=col...]
  transfers between devices with their start and end apart: 1 -> 1, of which waited for: 1 -> 1; matrix products, arithmetic and copies ran while one was open for 0% -> 0% of each run, Pallas kernels for 24% -> 25%
where the time goes in v5:
time: 19.8 us; the launch traced here: 19.6 us
  Pallas kernels  9.53 us (48%)
  starting transfers between devices  7.3 us (37%)
  waiting for transfers between devices  2.68 us (14%)
    all_to_all x1, starting transfers between devices, dense_shards(): lax.all_to_all(outgoing, ('rows', 'cols'), split_axis=0, concat_axis=0, t...  7.3 us
    pallas_call x1, Pallas kernels, dense_shards(): pl.pallas_call(spread_kernel, out_shape=(pltpu.VMEM((positions, users), j...  4.8 us
    pallas_call x1, Pallas kernels, dense_shards(): pl.pallas_call(functools.partial(solve_kernel, slots=slots, col_count=col...  2.86 us
    all_to_all x1, waiting for transfers between devices, dense_shards(): lax.all_to_all(outgoing, ('rows', 'cols'), split_axis=0, concat_axis=0, t...  2.68 us
    pallas_call x1, Pallas kernels, dense_shards(): pl.pallas_call(functools.partial(pick_kernel, col_count), out_shape=jax.S...  1.87 us
  transfers between devices with their start and end apart: 1, of which 1 were waited for; matrix products, arithmetic and copies ran while one was open for 0% of the time, Pallas kernels for 25%

profile of v5, /device:TPU:0, one launch (start us, length us, event | category | flops | bytes accessed | tf_op | source)
XLA Modules:
  0.0 19.6 jit_solution(10090981459528322074)
XLA Ops:
  0.0 1.9 %pick.1 = bf16[256,128]{1,0:T(8,128)(2,1)} custom-call(bf16[32,2048]{1,0:T(8,128)(2,1)} %factors_ref.1, s32[1,8,32]{2,1,0:T(8,128)} %list_ref.1), custom_call_target="tpu_custom_call" | custom-call | tf_op jit(solution)/shard_map/pick/pallas_call | solution.py:293
  1.9 0.0 copy-start
  1.9 7.3 %all-to-all-start = ((bf16[32,8,128]{2,1,0:T(8,128)(2,1)}), bf16[32,8,128]{2,1,0:T(8,128)(2,1)S(1)}, u32[]{:S(2)}, u32[]{:S(2)}) async-start(bf16[32,8,128]{2,1,0:T(8,128)(2,1)} %bitcast), calls=%async_computation | async-start | bytes 131072 | tf_op jit(solution)/shard_map/all_to_all | solution.py:308
  9.2 0.0 copy-done
  9.2 4.8 %spread.1 = (f32[256,1024]{1,0:T(8,128)S(1)}, bf16[512,1024]{1,0:T(8,128)(2,1)S(1)}) custom-call(s32[64,1024]{1,0:T(8,128)} %slot_hbm.1, f32[64,1024]{1,0:T(8,128)} %weight_hbm.1, f32[64,1024]{1,0:T(8,128)} %rating_hbm.1, s32[1,1024]{1,0:T(1,128)S(1)} %bitcast.4), custom_call_target="tpu_custom_call" | custom-call | flops 50331648 | bytes 2883584 | tf_op jit(solution)/shard_map/spread/pallas_call | solution.py:310
  14.0 2.7 %all-to-all-done = bf16[32,8,128]{2,1,0:T(8,128)(2,1)S(1)} async-done(((bf16[32,8,128]{2,1,0:T(8,128)(2,1)}), bf16[32,8,128]{2,1,0:T(8,128)(2,1)S(1)}, u32[]{:S(2)}, u32[]{:S(2)}) %all-to-all-start) | async-done | bytes 65568 | tf_op jit(solution)/shard_map/all_to_all | solution.py:308
  16.7 2.9 %solve.1 = f32[32,1024]{1,0:T(8,128)} custom-call(bf16[256,128]{1,0:T(8,128)(2,1)S(1)} %bitcast.3, f32[256,1024]{1,0:T(8,128)S(1)} %get-tuple-element.7.w_ref, bf16[512,1024]{1,0:T(8,128)(2,1)S(1)} %get-tuple-element.8.b_ref), custom_call_target="tpu_custom_call" | custom-call | tf_op jit(solution)/shard_map/solve/pallas_call | solution.py:332
Async XLA Ops:
  1.9 7.3 %copy-start = (s32[1024]{0:T(1024)S(1)}, s32[1024]{0:T(1024)}, u32[]{:S(2)}) copy-start(s32[1024]{0:T(1024)} %param.11) | copy-start | bytes 12292
  1.9 14.8 %all-to-all-start = ((bf16[32,8,128]{2,1,0:T(8,128)(2,1)}), bf16[32,8,128]{2,1,0:T(8,128)(2,1)S(1)}, u32[]{:S(2)}, u32[]{:S(2)}) async-start(bf16[32,8,128]{2,1,0:T(8,128)(2,1)} %bitcast), calls=%async_computation | async-start | bytes 131072 | tf_op jit(solution)/shard_map/all_to_all | solution.py:308

commit v6 on v5

--- a/solution.py
+++ b/solution.py
@@ -97,14 +97,22 @@
     factor_count, items = factors.shape
     _, row_count, slots = wanted.shape
     list_copy = pltpu.make_async_copy(list_ref, wanted, arrived.at[0])
-    factors_copy = pltpu.make_async_copy(factors_ref, factors, arrived.at[1])
+    quarter = items // 4
+    factors_copies = []
+    for part in range(4):
+        lanes = pl.ds(quarter * part, quarter)
+        factors_copies.append(
+            pltpu.make_async_copy(factors_ref.at[:, lanes], factors.at[:, lanes], arrived.at[1 + part])
+        )
     list_copy.start()
-    factors_copy.start()
+    for copy in factors_copies:
+        copy.start()
     within = lax.broadcasted_iota(jnp.int32, (128, row_count * slots), 0)
     list_copy.wait()
     item = jnp.concatenate([wanted[0, d : d + 1, :] for d in range(row_count)], axis=1)
     chosen = jnp.where(within == (item & 127), jnp.float32(1), jnp.float32(0)).astype(jnp.bfloat16)
-    factors_copy.wait()
+    for copy in factors_copies:
+        copy.wait()
     groups = items // 128
     stacked = jnp.concatenate([factors[:, 128 * g : 128 * (g + 1)] for g in range(groups)], axis=0)
     found = jnp.dot(stacked, chosen, preferred_element_type=jnp.float32)
@@ -120,16 +128,19 @@
         for d, chunk in enumerate(swap_blocks(parts, slots, per_tile), first):
             chunk = jnp.concatenate([chunk] * col_count, axis=0).astype(jnp.bfloat16)
             ready[chunk_rows * d : chunk_rows * (d + 1), :] = chunk
-        part = pl.ds(chunk_rows * first, chunk_rows * per_tile)
-        copy = pltpu.make_async_copy(ready.at[part], out_ref.at[part], left.at[len(copies)])
-        copy.start()
-        copies.append(copy)
+        half = chunk_rows * per_tile // 2
+        for start in (chunk_rows * first, chunk_rows * first + half):
+            part = pl.ds(start, half)
+            copy = pltpu.make_async_copy(ready.at[part], out_ref.at[part], left.at[len(copies)])
+            copy.start()
+            copies.append(copy)
     for copy in copies:
         copy.wait()
 
 
 def spread_kernel(
-    slot_hbm, weight_hbm, rating_hbm, counts_ref, w_ref, b_ref, slot_ref, weight_ref, rating_ref, wanted, named, arrived
+    slot_hbm, weight_hbm, rating_hbm, counts_hbm, w_ref, b_ref,
+    slot_ref, weight_ref, rating_ref, counts_ref, wanted, named, arrived
 ):
     obs, users = slot_ref.shape
     positions = w_ref.shape[0]
@@ -139,7 +150,7 @@
     copies = [
         pltpu.make_async_copy(source, target, arrived.at[at])
         for at, (source, target) in enumerate(
-            ((slot_hbm, slot_ref), (weight_hbm, weight_ref), (rating_hbm, rating_ref))
+            ((slot_hbm, slot_ref), (weight_hbm, weight_ref), (rating_hbm, rating_ref), (counts_hbm, counts_ref))
         )
     ]
     for copy in copies:
@@ -299,8 +310,8 @@
             pltpu.VMEM(item_factors.shape, item_factors.dtype),
             pltpu.VMEM(send_list.shape, send_list.dtype),
             pltpu.VMEM((chunk_rows, 128), jnp.bfloat16),
-            pltpu.SemaphoreType.DMA((2,)),
-            pltpu.SemaphoreType.DMA((positions // 128,)),
+            pltpu.SemaphoreType.DMA((5,)),
+            pltpu.SemaphoreType.DMA((2 * positions // 128,)),
         ],
         compiler_params=pltpu.CompilerParams(vmem_limit_bytes=4 << 20),
         name="pick",
@@ -313,22 +324,23 @@
             pltpu.VMEM((positions, users), jnp.float32),
             pltpu.VMEM((2 * positions, users), jnp.bfloat16),
         ),
-        in_specs=[hbm] * 3 + [vmem],
+        in_specs=[hbm] * 4,
         out_specs=[vmem] * 2,
         scratch_shapes=[
             pltpu.VMEM((obs, users), jnp.int32),
             pltpu.VMEM((obs, users), jnp.float32),
             pltpu.VMEM((obs, users), jnp.float32),
+            pltpu.VMEM((1, users), jnp.int32),
             pltpu.VMEM((32 * obs, 128), jnp.int8),
             pltpu.VMEM((positions, users), jnp.int8),
-            pltpu.SemaphoreType.DMA((3,)),
+            pltpu.SemaphoreType.DMA((4,)),
         ],
         compiler_params=pltpu.CompilerParams(vmem_limit_bytes=8 << 20),
         cost_estimate=pl.CostEstimate(
             flops=3 * obs * positions * users, bytes_accessed=(12 * obs + 8 * positions) * users, transcendentals=0
         ),
         name="spread",
-    )(*map(in_hbm, (obs_slot, obs_weight, rating)), counts)
+    )(*map(in_hbm, (obs_slot, obs_weight, rating, counts)))
     return pl.pallas_call(
         functools.partial(solve_kernel, slots=slots, col_count=col_count),
         out_shape=jax.ShapeDtypeStruct((own, users), jnp.float32),

time: 19.8 us -> 19.7 us (level)
  no operation moved by 1% of the time
where the time goes in v6:
time: 19.7 us; the launch traced here: 19.5 us
  Pallas kernels  9.48 us (48%)
  starting transfers between devices  7.31 us (37%)
  waiting for transfers between devices  2.68 us (14%)
    all_to_all x1, starting transfers between devices, dense_shards(): lax.all_to_all(outgoing, ('rows', 'cols'), split_axis=0, concat_axis=0, t...  7.31 us
    pallas_call x1, Pallas kernels, dense_shards(): pl.pallas_call(spread_kernel, out_shape=(pltpu.VMEM((positions, users), j...  4.81 us
    pallas_call x1, Pallas kernels, dense_shards(): pl.pallas_call(functools.partial(solve_kernel, slots=slots, col_count=col...  2.86 us
    all_to_all x1, waiting for transfers between devices, dense_shards(): lax.all_to_all(outgoing, ('rows', 'cols'), split_axis=0, concat_axis=0, t...  2.68 us
    pallas_call x1, Pallas kernels, dense_shards(): pl.pallas_call(functools.partial(pick_kernel, col_count), out_shape=jax.S...  1.81 us
  transfers between devices with their start and end apart: 1, of which 1 were waited for; matrix products, arithmetic and copies ran while one was open for 0% of the time, Pallas kernels for 25%

profile of v6, /device:TPU:0, one launch (start us, length us, event | category | flops | bytes accessed | tf_op | source)
XLA Modules:
  0.0 19.5 jit_solution(12648184420439306430)
XLA Ops:
  0.0 1.8 %pick.1 = bf16[256,128]{1,0:T(8,128)(2,1)} custom-call(bf16[32,2048]{1,0:T(8,128)(2,1)} %factors_ref.1, s32[1,8,32]{2,1,0:T(8,128)} %list_ref.1), custom_call_target="tpu_custom_call" | custom-call | tf_op jit(solution)/shard_map/pick/pallas_call | solution.py:304
  1.8 7.3 %all-to-all-start = ((bf16[32,8,128]{2,1,0:T(8,128)(2,1)}), bf16[32,8,128]{2,1,0:T(8,128)(2,1)S(1)}, u32[]{:S(2)}, u32[]{:S(2)}) async-start(bf16[32,8,128]{2,1,0:T(8,128)(2,1)} %bitcast), calls=%async_computation | async-start | bytes 131072 | tf_op jit(solution)/shard_map/all_to_all | solution.py:319
  9.1 4.8 %spread.1 = (f32[256,1024]{1,0:T(8,128)S(1)}, bf16[512,1024]{1,0:T(8,128)(2,1)S(1)}) custom-call(s32[64,1024]{1,0:T(8,128)} %slot_hbm.1, f32[64,1024]{1,0:T(8,128)} %weight_hbm.1, f32[64,1024]{1,0:T(8,128)} %rating_hbm.1, s32[1,1024]{1,0:T(1,128)} %bitcast.4), custom_call_target="tpu_custom_call" | custom-call | flops 50331648 | bytes 2883584 | tf_op jit(solution)/shard_map/spread/pallas_call | solution.py:321
  14.0 2.7 %all-to-all-done = bf16[32,8,128]{2,1,0:T(8,128)(2,1)S(1)} async-done(((bf16[32,8,128]{2,1,0:T(8,128)(2,1)}), bf16[32,8,128]{2,1,0:T(8,128)(2,1)S(1)}, u32[]{:S(2)}, u32[]{:S(2)}) %all-to-all-start) | async-done | bytes 65568 | tf_op jit(solution)/shard_map/all_to_all | solution.py:319
  16.6 2.9 %solve.1 = f32[32,1024]{1,0:T(8,128)} custom-call(bf16[256,128]{1,0:T(8,128)(2,1)S(1)} %bitcast.3, f32[256,1024]{1,0:T(8,128)S(1)} %get-tuple-element.7.w_ref, bf16[512,1024]{1,0:T(8,128)(2,1)S(1)} %get-tuple-element.8.b_ref), custom_call_target="tpu_custom_call" | custom-call | tf_op jit(solution)/shard_map/solve/pallas_call | solution.py:344
Async XLA Ops:
  1.8 14.8 %all-to-all-start = ((bf16[32,8,128]{2,1,0:T(8,128)(2,1)}), bf16[32,8,128]{2,1,0:T(8,128)(2,1)S(1)}, u32[]{:S(2)}, u32[]{:S(2)}) async-start(bf16[32,8,128]{2,1,0:T(8,128)(2,1)} %bitcast), calls=%async_computation | async-start | bytes 131072 | tf_op jit(solution)/shard_map/all_to_all | solution.py:319

commit v7 on v6

--- a/solution.py
+++ b/solution.py
@@ -251,8 +251,11 @@
         parts = [slice(at, at + 128) for at in range(0, positions, 128)]
         return [(along[part], w_ref[part, lanes] * along[part]) for part in parts]
 
-    def square(views):
-        return sum(total(scaled * along) for along, scaled in views)
+    def square(lanes, direction):
+        pieces = pieces_of(direction, 2)
+        parts = [slice(at, at + 128) for at in range(0, positions, 128)]
+        views = [(dot(twice_t[part], pieces), w_ref[part, lanes]) for part in parts]
+        return sum(total(weight * along * along) for along, weight in views)
 
     def back(lanes, views, direction):
         pieces = jnp.concatenate([pieces_of(scaled, 2) for _, scaled in views], axis=0)
@@ -283,7 +286,7 @@
         images = [back(lanes, look(lanes, state[1]), state[1]) for lanes, state in zip(groups, states)]
         states = [advance(state, image) for state, image in zip(states, images)]
     for lanes, state in zip(groups, states):
-        finish(lanes, state, square(look(lanes, state[1])))
+        finish(lanes, state, square(lanes, state[1]))
 
 
 def dense_shards(item_factors, send_list, obs_slot, obs_weight, rating, counts):

time: 19.7 us -> 19.8 us (level)
  no operation moved by 1% of the time
where the time goes in v7:
time: 19.8 us; the launch traced here: 19.5 us
  Pallas kernels  9.51 us (48%)
  starting transfers between devices  7.31 us (37%)
  waiting for transfers between devices  2.68 us (14%)
    all_to_all x1, starting transfers between devices, dense_shards(): lax.all_to_all(outgoing, ('rows', 'cols'), split_axis=0, concat_axis=0, t...  7.31 us
    pallas_call x1, Pallas kernels, dense_shards(): pl.pallas_call(spread_kernel, out_shape=(pltpu.VMEM((positions, users), j...  4.81 us
    pallas_call x1, Pallas kernels, dense_shards(): pl.pallas_call(functools.partial(solve_kernel, slots=slots, col_count=col...  2.88 us
    all_to_all x1, waiting for transfers between devices, dense_shards(): lax.all_to_all(outgoing, ('rows', 'cols'), split_axis=0, concat_axis=0, t...  2.68 us
    pallas_call x1, Pallas kernels, dense_shards(): pl.pallas_call(functools.partial(pick_kernel, col_count), out_shape=jax.S...  1.81 us
  transfers between devices with their start and end apart: 1, of which 1 were waited for; matrix products, arithmetic and copies ran while one was open for 0% of the time, Pallas kernels for 25%

profile of v7, /device:TPU:0, one launch (start us, length us, event | category | flops | bytes accessed | tf_op | source)
XLA Modules:
  0.0 19.5 jit_solution(1951306911712774872)
XLA Ops:
  0.0 1.8 %pick.1 = bf16[256,128]{1,0:T(8,128)(2,1)} custom-call(bf16[32,2048]{1,0:T(8,128)(2,1)} %factors_ref.1, s32[1,8,32]{2,1,0:T(8,128)} %list_ref.1), custom_call_target="tpu_custom_call" | custom-call | tf_op jit(solution)/shard_map/pick/pallas_call | solution.py:307
  1.8 7.3 %all-to-all-start = ((bf16[32,8,128]{2,1,0:T(8,128)(2,1)}), bf16[32,8,128]{2,1,0:T(8,128)(2,1)S(1)}, u32[]{:S(2)}, u32[]{:S(2)}) async-start(bf16[32,8,128]{2,1,0:T(8,128)(2,1)} %bitcast), calls=%async_computation | async-start | bytes 131072 | tf_op jit(solution)/shard_map/all_to_all | solution.py:322
  9.1 4.8 %spread.1 = (f32[256,1024]{1,0:T(8,128)S(1)}, bf16[512,1024]{1,0:T(8,128)(2,1)S(1)}) custom-call(s32[64,1024]{1,0:T(8,128)} %slot_hbm.1, f32[64,1024]{1,0:T(8,128)} %weight_hbm.1, f32[64,1024]{1,0:T(8,128)} %rating_hbm.1, s32[1,1024]{1,0:T(1,128)} %bitcast.4), custom_call_target="tpu_custom_call" | custom-call | flops 50331648 | bytes 2883584 | tf_op jit(solution)/shard_map/spread/pallas_call | solution.py:324
  14.0 2.7 %all-to-all-done = bf16[32,8,128]{2,1,0:T(8,128)(2,1)S(1)} async-done(((bf16[32,8,128]{2,1,0:T(8,128)(2,1)}), bf16[32,8,128]{2,1,0:T(8,128)(2,1)S(1)}, u32[]{:S(2)}, u32[]{:S(2)}) %all-to-all-start) | async-done | bytes 65568 | tf_op jit(solution)/shard_map/all_to_all | solution.py:322
  16.6 2.9 %solve.1 = f32[32,1024]{1,0:T(8,128)} custom-call(bf16[256,128]{1,0:T(8,128)(2,1)S(1)} %bitcast.3, f32[256,1024]{1,0:T(8,128)S(1)} %get-tuple-element.7.w_ref, bf16[512,1024]{1,0:T(8,128)(2,1)S(1)} %get-tuple-element.8.b_ref), custom_call_target="tpu_custom_call" | custom-call | tf_op jit(solution)/shard_map/solve/pallas_call | solution.py:347
Async XLA Ops:
  1.8 14.8 %all-to-all-start = ((bf16[32,8,128]{2,1,0:T(8,128)(2,1)}), bf16[32,8,128]{2,1,0:T(8,128)(2,1)S(1)}, u32[]{:S(2)}, u32[]{:S(2)}) async-start(bf16[32,8,128]{2,1,0:T(8,128)(2,1)} %bitcast), calls=%async_computation | async-start | bytes 131072 | tf_op jit(solution)/shard_map/all_to_all | solution.py:322

commit v8 on v7

--- a/solution.py
+++ b/solution.py
@@ -244,7 +244,8 @@
         return jnp.sum(values, axis=0, keepdims=True)
 
     def target(lanes):
-        return dot(twice[...], b_ref[:, lanes])
+        parts = [slice(at, at + 256) for at in range(0, 2 * positions, 256)]
+        return sum(dot(twice[:, part], b_ref[part, lanes]) for part in parts)
 
     def look(lanes, direction):
         along = dot(twice_t[...], pieces_of(direction, 2))

time: 19.8 us -> 19.8 us (level)
  no operation moved by 1% of the time
where the time goes in v8:
time: 19.8 us; the launch traced here: 19.5 us
  Pallas kernels  9.51 us (48%)
  starting transfers between devices  7.31 us (37%)
  waiting for transfers between devices  2.68 us (14%)
    all_to_all x1, starting transfers between devices, dense_shards(): lax.all_to_all(outgoing, ('rows', 'cols'), split_axis=0, concat_axis=0, t...  7.31 us
    pallas_call x1, Pallas kernels, dense_shards(): pl.pallas_call(spread_kernel, out_shape=(pltpu.VMEM((positions, users), j...  4.81 us
    pallas_call x1, Pallas kernels, dense_shards(): pl.pallas_call(functools.partial(solve_kernel, slots=slots, col_count=col...  2.89 us
    all_to_all x1, waiting for transfers between devices, dense_shards(): lax.all_to_all(outgoing, ('rows', 'cols'), split_axis=0, concat_axis=0, t...  2.68 us
    pallas_call x1, Pallas kernels, dense_shards(): pl.pallas_call(functools.partial(pick_kernel, col_count), out_shape=jax.S...  1.81 us
  transfers between devices with their start and end apart: 1, of which 1 were waited for; matrix products, arithmetic and copies ran while one was open for 0% of the time, Pallas kernels for 25%

profile of v8, /device:TPU:0, one launch (start us, length us, event | category | flops | bytes accessed | tf_op | source)
XLA Modules:
  0.0 19.5 jit_solution(14722406533797003008)
XLA Ops:
  0.0 1.8 %pick.1 = bf16[256,128]{1,0:T(8,128)(2,1)} custom-call(bf16[32,2048]{1,0:T(8,128)(2,1)} %factors_ref.1, s32[1,8,32]{2,1,0:T(8,128)} %list_ref.1), custom_call_target="tpu_custom_call" | custom-call | tf_op jit(solution)/shard_map/pick/pallas_call | solution.py:308
  1.8 7.3 %all-to-all-start = ((bf16[32,8,128]{2,1,0:T(8,128)(2,1)}), bf16[32,8,128]{2,1,0:T(8,128)(2,1)S(1)}, u32[]{:S(2)}, u32[]{:S(2)}) async-start(bf16[32,8,128]{2,1,0:T(8,128)(2,1)} %bitcast), calls=%async_computation | async-start | bytes 131072 | tf_op jit(solution)/shard_map/all_to_all | solution.py:323
  9.1 4.8 %spread.1 = (f32[256,1024]{1,0:T(8,128)S(1)}, bf16[512,1024]{1,0:T(8,128)(2,1)S(1)}) custom-call(s32[64,1024]{1,0:T(8,128)} %slot_hbm.1, f32[64,1024]{1,0:T(8,128)} %weight_hbm.1, f32[64,1024]{1,0:T(8,128)} %rating_hbm.1, s32[1,1024]{1,0:T(1,128)} %bitcast.4), custom_call_target="tpu_custom_call" | custom-call | flops 50331648 | bytes 2883584 | tf_op jit(solution)/shard_map/spread/pallas_call | solution.py:325
  14.0 2.7 %all-to-all-done = bf16[32,8,128]{2,1,0:T(8,128)(2,1)S(1)} async-done(((bf16[32,8,128]{2,1,0:T(8,128)(2,1)}), bf16[32,8,128]{2,1,0:T(8,128)(2,1)S(1)}, u32[]{:S(2)}, u32[]{:S(2)}) %all-to-all-start) | async-done | bytes 65568 | tf_op jit(solution)/shard_map/all_to_all | solution.py:323
  16.6 2.9 %solve.1 = f32[32,1024]{1,0:T(8,128)} custom-call(bf16[256,128]{1,0:T(8,128)(2,1)S(1)} %bitcast.3, f32[256,1024]{1,0:T(8,128)S(1)} %get-tuple-element.7.w_ref, bf16[512,1024]{1,0:T(8,128)(2,1)S(1)} %get-tuple-element.8.b_ref), custom_call_target="tpu_custom_call" | custom-call | tf_op jit(solution)/shard_map/solve/pallas_call | solution.py:348
Async XLA Ops:
  1.8 14.8 %all-to-all-start = ((bf16[32,8,128]{2,1,0:T(8,128)(2,1)}), bf16[32,8,128]{2,1,0:T(8,128)(2,1)S(1)}, u32[]{:S(2)}, u32[]{:S(2)}) async-start(bf16[32,8,128]{2,1,0:T(8,128)(2,1)} %bitcast), calls=%async_computation | async-start | bytes 131072 | tf_op jit(solution)/shard_map/all_to_all | solution.py:323
